TPU v7x, 32 devices: a whole 2x2x4 slice. The times are simulated.
32 devices in a mesh: pairs: 8 (over z, x), tm: 4 (over y, core).
Axes of the slice: x: 2, y: 2, z: 4, core: 2. Of those that a mesh axis runs over, the one named last changes fastest.
Arguments:
- traces: float32 [8, 512, 6144], P('tm', 'pairs'), may hold values from -64 to 64
- station_slot: int32 [512], replicated, may hold values from 0 to 511, as said below
- pair_stations: int32 [512, 2], P('pairs'), may hold values from 0 to 511, as said below
Outputs:
- correlation_stack: float32 [2048, 512], P('tm', 'pairs')
Inputs may be any that keep to these rules, and one draw needn't show every extreme that they name: `station_slot`: A permutation: rows r * 64 to (r + 1) * 64 - 1 of traces are the stations of owner r. `pair_stations`: in each block of 64 pairs (the pairs of one device), at most 32 of the 128 pair ends name stations whose station_slot // 64 is one value, and in every block one value is named by exactly 32 ends. A pair may name one station twice.
All inputs are finite; a program needn't handle non-finite values.
Results may differ from a plain program's by a relative error of at most 0.011.
Values may be sent and summed in bfloat16 or wider, within the bound.
A program may use at most 64 MiB of HBM per device.

v0:
```python
import math

import jax
import jax.numpy as jnp
from jax import lax
from jax.sharding import PartitionSpec as P

F = 1536
FLO = 32
LAG = 1024


two_pi = 6.283185307179586


def tapered_rows(traces):
    length = traces.shape[-1]
    sample_times = lax.iota(jnp.int32, length).astype(jnp.float32)
    hann_window = 0.5 - 0.5 * jnp.cos((sample_times + 0.5) * (two_pi / length))
    centred = traces - jnp.mean(traces, axis=-1, keepdims=True)
    return (centred * hann_window).astype(jnp.bfloat16)


def forward_table(first_row, row_count, length, first_bin, bins):
    sample_times = first_row + lax.iota(jnp.int32, row_count)
    frequencies = first_bin + lax.iota(jnp.int32, bins)
    phases = sample_times[:, None] * frequencies[None, :] % length
    angles = phases.astype(jnp.float32) * (two_pi / length)
    return jnp.concatenate([jnp.cos(angles), -jnp.sin(angles)], axis=1).astype(jnp.bfloat16)


def whiten(spectrum, bins):
    real_part = spectrum[..., :bins]
    imag_part = spectrum[..., bins:]
    energy = real_part * real_part + imag_part * imag_part
    water_level = jnp.mean(energy, axis=-1, keepdims=True)
    scaling = lax.rsqrt(energy + 0.1 * water_level + 1e-06)
    return jnp.concatenate([real_part * scaling, imag_part * scaling], axis=-1).astype(jnp.bfloat16)


def whiten_spectra(tapered, first_bin, bins):
    length = tapered.shape[1]
    block_rows = min(512, length)

    def add_block(step_index, running):
        first_row = step_index * block_rows
        segment = lax.dynamic_slice_in_dim(tapered, first_row, block_rows, 1)
        cos_table = forward_table(first_row, block_rows, length, first_bin, bins)
        return running + jnp.dot(segment, cos_table, preferred_element_type=jnp.float32)

    spectrum = lax.fori_loop(
        0, length // block_rows, add_block, jnp.zeros((tapered.shape[0], 2 * bins), jnp.float32)
    )
    return whiten(spectrum, bins)


def cross_spectra(left_ends, right_ends, bins):
    left_real = left_ends[..., :bins].astype(jnp.float32)
    left_imag = left_ends[..., bins:].astype(jnp.float32)
    right_real = right_ends[..., :bins].astype(jnp.float32)
    right_imag = right_ends[..., bins:].astype(jnp.float32)
    return jnp.concatenate(
        [
            left_real * right_real + left_imag * right_imag,
            left_imag * right_real - left_real * right_imag,
        ],
        axis=-1,
    )


def lag_block(stacked, first_row, row_count, first_bin, bins, length, half_span):
    lag_values = first_row + lax.iota(jnp.int32, row_count) - half_span
    frequencies = first_bin + lax.iota(jnp.int32, bins)
    phases = lag_values[:, None] * frequencies[None, :] % length
    angles = phases.astype(jnp.float32) * (two_pi / length)
    lag_table = jnp.concatenate([jnp.cos(angles), -jnp.sin(angles)], axis=1)
    return lax.dot_general(
        lag_table,
        stacked,
        (((1,), (1,)), ((), ())),
        precision=lax.Precision.HIGHEST,
        preferred_element_type=jnp.float32,
    )


def lag_rows(stacked, first_row, row_count, block_rows, length):

    def one_block(block_index):
        return lag_block(
            stacked, first_row + block_index * block_rows, block_rows, FLO, F, length, LAG
        )

    pieces = lax.map(one_block, jnp.arange(row_count // block_rows, dtype=jnp.int32))
    return pieces.reshape(row_count, stacked.shape[0])


def on_device(traces, station_slot, pair_stations):
    window_count, station_count, length = traces.shape
    pair_count = pair_stations.shape[0]
    blocks = lax.axis_size("pairs")
    capacity = 4 * pair_count // blocks
    own_index = lax.axis_index("pairs")
    every_pair = lax.all_gather(pair_stations, "pairs", axis=0, tiled=True)
    slot_ids = station_slot[every_pair.reshape(blocks, 2 * pair_count)]
    owners = slot_ids // station_count
    local_rows = slot_ids % station_count
    onehot = (owners[:, :, None] == lax.iota(jnp.int32, blocks)[None, None, :]).astype(jnp.int32)
    end_ranks = jnp.sum((jnp.cumsum(onehot, axis=1) - onehot) * onehot, axis=2)
    wanted = (owners == own_index)[:, :, None] & (
        end_ranks[:, :, None] == lax.iota(jnp.int32, capacity)[None, None, :]
    )
    send_rows = jnp.sum(jnp.where(wanted, local_rows[:, :, None], 0), axis=1)
    own_owners = lax.dynamic_index_in_dim(owners, own_index, 0, keepdims=False)
    own_ranks = lax.dynamic_index_in_dim(end_ranks, own_index, 0, keepdims=False)
    positions = own_owners * capacity + own_ranks
    tapered = tapered_rows(traces).reshape(window_count * station_count, length)
    spectra = whiten_spectra(tapered, FLO, F).reshape(window_count, station_count, 2 * F)
    received = lax.all_to_all(
        spectra[:, send_rows], "pairs", split_axis=1, concat_axis=1, tiled=True
    )
    held_windows = received.shape[0]
    flattened = received.reshape(held_windows, blocks * capacity, 2 * F)
    pair_ends = flattened[:, positions].reshape(held_windows, pair_count, 2, 2 * F)
    cross_terms = cross_spectra(pair_ends[:, :, 0], pair_ends[:, :, 1], F)
    stacked = jnp.sum(cross_terms, axis=0)
    lag_share = 2 * LAG // lax.axis_size("tm")
    normalizer = 1.0 / math.sqrt(F * window_count * lax.axis_size("tm"))
    block_rows = min(256, lag_share)
    summed = lax.psum(stacked, "tm")
    correlation_stack = (
        lag_rows(summed, lax.axis_index("tm") * lag_share, lag_share, block_rows, length)
        * normalizer
    )
    return correlation_stack


def solution(mesh):
    in_specs = (P("tm", "pairs", None), P(), P("pairs", None))
    out_specs = P("tm", "pairs")
    return jax.shard_map(
        on_device, mesh=mesh, in_specs=in_specs, out_specs=out_specs, check_vma=False
    )
```

profile of v0, /device:TPU:0, one launch (start us, length us, event | category | flops | bytes accessed | tf_op | source)
XLA Modules:
  0.0 404.0 jit_solution(17786548963787513633)
XLA Ops:
  11.0 201.3 %while.29 = (s32[]{:T(128)}, f32[128,3072]{1,0:T(8,128)}, bf16[128,6144]{1,0:T(8,128)(2,1)}, s32[]{:T(128)}, s32[]{:T(128)}, /*index=5*/s32[]{:T(128)}, s32[]{:T(128)}) while((s32[]{:T(128)}, f32[128,3072]{1,0:T(8,128)}, bf16[128,6144]{1,0:T(8,128)(2,1)}, s32[]{:T(128)}, s32[]{:T(128)}, /*index=5*/s32[]{:T(128)}, s32[]{:T(128)}) %tuple.80), condition=%wide.region_2.3_spmd.clone, body=%wide.region_1.2_spmd.clone.sunk | while | flops 419170304 | bytes 9584781 | solution.py:51
  11.0 13.5 %cosine_convert_fusion.2 = (bf16[512,1536]{1,0:T(8,128)(2,1)S(1)}, bf16[512,1536]{1,0:T(8,128)(2,1)S(1)}) fusion(s32[1536]{0:T(1024)S(1)} %iota_add_fusion.7, s32[512]{0:T(512)S(1)} %iota_add_fusion.8), kind=kLoop, calls=%fused_computation.29.clone.1 | loop fusion | flops 9437184 | bytes 3153920 | tf_op jit(solution)/shard_map/convert
  27.3 13.5 %cosine_convert_fusion.2 = (bf16[512,1536]{1,0:T(8,128)(2,1)S(1)}, bf16[512,1536]{1,0:T(8,128)(2,1)S(1)}) fusion(s32[1536]{0:T(1024)S(1)} %iota_add_fusion.7, s32[512]{0:T(512)S(1)} %iota_add_fusion.8), kind=kLoop, calls=%fused_computation.29.clone.1 | loop fusion | flops 9437184 | bytes 3153920 | tf_op jit(solution)/shard_map/convert
  40.8 3.3 convolution_add_fusion.2
  44.1 13.5 %cosine_convert_fusion.2 = (bf16[512,1536]{1,0:T(8,128)(2,1)S(1)}, bf16[512,1536]{1,0:T(8,128)(2,1)S(1)}) fusion(s32[1536]{0:T(1024)S(1)} %iota_add_fusion.7, s32[512]{0:T(512)S(1)} %iota_add_fusion.8), kind=kLoop, calls=%fused_computation.29.clone.1 | loop fusion | flops 9437184 | bytes 3153920 | tf_op jit(solution)/shard_map/convert
  60.9 13.5 %cosine_convert_fusion.2 = (bf16[512,1536]{1,0:T(8,128)(2,1)S(1)}, bf16[512,1536]{1,0:T(8,128)(2,1)S(1)}) fusion(s32[1536]{0:T(1024)S(1)} %iota_add_fusion.7, s32[512]{0:T(512)S(1)} %iota_add_fusion.8), kind=kLoop, calls=%fused_computation.29.clone.1 | loop fusion | flops 9437184 | bytes 3153920 | tf_op jit(solution)/shard_map/convert
  74.5 3.3 convolution_add_fusion.2
  77.8 13.5 %cosine_convert_fusion.2 = (bf16[512,1536]{1,0:T(8,128)(2,1)S(1)}, bf16[512,1536]{1,0:T(8,128)(2,1)S(1)}) fusion(s32[1536]{0:T(1024)S(1)} %iota_add_fusion.7, s32[512]{0:T(512)S(1)} %iota_add_fusion.8), kind=kLoop, calls=%fused_computation.29.clone.1 | loop fusion | flops 9437184 | bytes 3153920 | tf_op jit(solution)/shard_map/convert
  91.3 3.3 convolution_add_fusion.2
  94.6 13.5 %cosine_convert_fusion.2 = (bf16[512,1536]{1,0:T(8,128)(2,1)S(1)}, bf16[512,1536]{1,0:T(8,128)(2,1)S(1)}) fusion(s32[1536]{0:T(1024)S(1)} %iota_add_fusion.7, s32[512]{0:T(512)S(1)} %iota_add_fusion.8), kind=kLoop, calls=%fused_computation.29.clone.1 | loop fusion | flops 9437184 | bytes 3153920 | tf_op jit(solution)/shard_map/convert
  108.1 3.3 convolution_add_fusion.2
  111.4 13.5 %cosine_convert_fusion.2 = (bf16[512,1536]{1,0:T(8,128)(2,1)S(1)}, bf16[512,1536]{1,0:T(8,128)(2,1)S(1)}) fusion(s32[1536]{0:T(1024)S(1)} %iota_add_fusion.7, s32[512]{0:T(512)S(1)} %iota_add_fusion.8), kind=kLoop, calls=%fused_computation.29.clone.1 | loop fusion | flops 9437184 | bytes 3153920 | tf_op jit(solution)/shard_map/convert
  124.9 3.3 convolution_add_fusion.2
  128.2 13.5 %cosine_convert_fusion.2 = (bf16[512,1536]{1,0:T(8,128)(2,1)S(1)}, bf16[512,1536]{1,0:T(8,128)(2,1)S(1)}) fusion(s32[1536]{0:T(1024)S(1)} %iota_add_fusion.7, s32[512]{0:T(512)S(1)} %iota_add_fusion.8), kind=kLoop, calls=%fused_computation.29.clone.1 | loop fusion | flops 9437184 | bytes 3153920 | tf_op jit(solution)/shard_map/convert
  141.8 3.3 convolution_add_fusion.2
  145.1 13.5 %cosine_convert_fusion.2 = (bf16[512,1536]{1,0:T(8,128)(2,1)S(1)}, bf16[512,1536]{1,0:T(8,128)(2,1)S(1)}) fusion(s32[1536]{0:T(1024)S(1)} %iota_add_fusion.7, s32[512]{0:T(512)S(1)} %iota_add_fusion.8), kind=kLoop, calls=%fused_computation.29.clone.1 | loop fusion | flops 9437184 | bytes 3153920 | tf_op jit(solution)/shard_map/convert
  158.6 3.3 convolution_add_fusion.2
  161.9 13.5 %cosine_convert_fusion.2 = (bf16[512,1536]{1,0:T(8,128)(2,1)S(1)}, bf16[512,1536]{1,0:T(8,128)(2,1)S(1)}) fusion(s32[1536]{0:T(1024)S(1)} %iota_add_fusion.7, s32[512]{0:T(512)S(1)} %iota_add_fusion.8), kind=kLoop, calls=%fused_computation.29.clone.1 | loop fusion | flops 9437184 | bytes 3153920 | tf_op jit(solution)/shard_map/convert
  178.7 13.5 %cosine_convert_fusion.2 = (bf16[512,1536]{1,0:T(8,128)(2,1)S(1)}, bf16[512,1536]{1,0:T(8,128)(2,1)S(1)}) fusion(s32[1536]{0:T(1024)S(1)} %iota_add_fusion.7, s32[512]{0:T(512)S(1)} %iota_add_fusion.8), kind=kLoop, calls=%fused_computation.29.clone.1 | loop fusion | flops 9437184 | bytes 3153920 | tf_op jit(solution)/shard_map/convert
  192.2 3.3 convolution_add_fusion.2
  195.5 13.5 %cosine_convert_fusion.2 = (bf16[512,1536]{1,0:T(8,128)(2,1)S(1)}, bf16[512,1536]{1,0:T(8,128)(2,1)S(1)}) fusion(s32[1536]{0:T(1024)S(1)} %iota_add_fusion.7, s32[512]{0:T(512)S(1)} %iota_add_fusion.8), kind=kLoop, calls=%fused_computation.29.clone.1 | loop fusion | flops 9437184 | bytes 3153920 | tf_op jit(solution)/shard_map/convert
  209.1 3.3 convolution_add_fusion.2
  215.4 22.4 %all-gather = s32[8,64,2]{1,2,0:T(2,128)S(1)} all-gather(s32[1,64,2]{1,2,0:T(2,128)S(1)} %bitcast.76), channel_id=1, replica_groups=mesh['pairs'=8,'tm'=4] {'pairs'}, dimensions={0}, use_global_device_ids=true | all-gather | bytes 4608 | tf_op jit(solution)/shard_map/all_gather | solution.py:103
  238.0 6.9 %gather_fusion = s32[1024]{0:T(1024)S(1)} fusion(s32[512]{0:T(512)S(1)} %copy-done, s32[1024]{0:T(1024)S(1)} %bitcast_clamp_fusion), kind=kCustom, calls=%fused_computation | custom fusion | bytes 12288 | tf_op jit(solution)/shard_map/gather | solution.py:104
  248.6 12.9 %gather_fusion.1 = bf16[256,2,3072]{2,1,0:T(2,128)(2,1)} fusion(bf16[2,64,3072]{2,0,1:T(2,128)(2,1)S(1)} %pad_maximum_fusion, s32[1024]{0:T(1024)S(1)} %pad_clamp_fusion.1), kind=kCustom, calls=%fused_computation.1 | custom fusion | bytes 6292480 | tf_op jit(solution)/shard_map/gather | solution.py:119
  261.5 3.6 all-to-all-start
  265.4 67.0 %all-to-all-done = bf16[2,8,32,3072]{3,0,2,1:T(2,128)(2,1)S(1)} async-done(((bf16[2,8,32,3072]{3,0,2,1:T(2,128)(2,1)}), bf16[2,8,32,3072]{3,0,2,1:T(2,128)(2,1)S(1)}, u32[]{:S(2)}, u32[]{:S(2)}) %all-to-all-start) | async-done | bytes 3145760 | tf_op jit(solution)/shard_map/all_to_all | solution.py:118
  332.5 4.8 %gather_fusion.2 = bf16[128,2,3072]{2,1,0:T(2,128)(2,1)} fusion(bf16[2,256,3072]{2,0,1:T(2,128)(2,1)S(1)} %bitcast.70, s32[1024]{0:T(1024)S(1)} %pad_clamp_fusion), kind=kCustom, calls=%fused_computation.2 | custom fusion | bytes 3146240 | tf_op jit(solution)/shard_map/gather | solution.py:123
  341.3 33.6 %all-reduce.2.cloned.1.call-done = f32[64,3072]{1,0:T(8,128)} async-done(((f32[64,3072]{1,0:T(8,128)}), f32[64,3072]{1,0:T(8,128)}) %all-reduce.2.cloned.1.call-update) | async-done | bytes 786448 | tf_op jit(solution)/shard_map/psum | solution.py:129
  374.9 21.5 %while.28 = (s32[]{:T(128)}, f32[2,256,64]{1,2,0:T(8,128)S(1)}, s32[2]{0:T(128)S(1)}, s32[]{:T(128)}, f32[64,3072]{1,0:T(8,128)}, /*index=5*/s32[]{:T(128)}, s32[1]{0:T(128)}) while((s32[]{:T(128)}, f32[2,256,64]{1,2,0:T(8,128)S(1)}, s32[2]{0:T(128)S(1)}, s32[]{:T(128)}, f32[64,3072]{1,0:T(8,128)}, /*index=5*/s32[]{:T(128)}, ...), condition=%wide.region_10.11_spmd, body=%wide.region_9.10_spmd.sunk | while | flops 608700416 | bytes 10303637 | solution.py:93
  376.3 6.4 %fusion.51 = (f32[256,1536]{1,0:T(8,128)S(1)}, f32[256,1536]{1,0:T(8,128)S(1)}) fusion(s32[1536]{0:T(1024)S(1)} %iota_add_fusion.6, s32[256]{0:T(256)S(1)} %add_add_fusion.2), kind=kLoop, calls=%fused_computation.14.clone.1 | loop fusion | flops 3932160 | bytes 3152896 | tf_op jit(solution)/shard_map/while/body/eval_jaxpr/cos | solution.py:76
  387.0 6.4 %fusion.51 = (f32[256,1536]{1,0:T(8,128)S(1)}, f32[256,1536]{1,0:T(8,128)S(1)}) fusion(s32[1536]{0:T(1024)S(1)} %iota_add_fusion.6, s32[256]{0:T(256)S(1)} %add_add_fusion.2), kind=kLoop, calls=%fused_computation.14.clone.1 | loop fusion | flops 3932160 | bytes 3152896 | tf_op jit(solution)/shard_map/while/body/eval_jaxpr/cos | solution.py:76
  (83 shorter events, 33.0 us)
Async XLA Ops:
  6.5 231.5 %copy-start = (s32[512]{0:T(512)S(1)}, s32[512]{0:T(512)}, u32[]{:S(2)}) copy-start(s32[512]{0:T(512)} %param.8) | copy-start | bytes 6148
  6.7 2.8 copy-start.2
  212.4 1.9 copy-start.3
  214.2 1.1 copy-start.4
  261.5 71.0 %all-to-all-start = ((bf16[2,8,32,3072]{3,0,2,1:T(2,128)(2,1)}), bf16[2,8,32,3072]{3,0,2,1:T(2,128)(2,1)S(1)}, u32[]{:S(2)}, u32[]{:S(2)}) async-start(bf16[2,8,32,3072]{3,0,2,1:T(2,128)(2,1)} %bitcast.69), calls=%async_computation | async-start | bytes 6291456 | tf_op jit(solution)/shard_map/all_to_all | solution.py:118
  265.1 109.8 %all-reduce.2.cloned.1.call-start = ((), (), s32[]{:S(2)}) async-start(), calls=%async_computation.1 | async-start | bytes 1572864 | tf_op jit(solution)/shard_map/psum | solution.py:129
  376.3 6.4 %copy-start.1 = (f32[64,3072]{1,0:T(8,128)S(1)}, f32[64,3072]{1,0:T(8,128)}, u32[]{:S(2)}) copy-start(f32[64,3072]{1,0:T(8,128)} %get-tuple-element.302) | copy-start | bytes 2359300 | tf_op jit(solution)/shard_map/while
  387.0 6.4 %copy-start.1 = (f32[64,3072]{1,0:T(8,128)S(1)}, f32[64,3072]{1,0:T(8,128)}, u32[]{:S(2)}) copy-start(f32[64,3072]{1,0:T(8,128)} %get-tuple-element.302) | copy-start | bytes 2359300 | tf_op jit(solution)/shard_map/while
Sparse Core Ops, SparseCore 0:
  341.4 33.4 all-reduce.1
where the time goes:
time: 405 us; the launch traced here: 404 us
  other arithmetic  186 us (46%)
  waiting for transfers between devices  101 us (25%)
  matrix products  44.8 us (11%)
  local copies, waits for them, and re-layouts  31.2 us (8%)
  blocking collectives  22.4 us (6%)
  between operations  13.6 us (3%)
    another operation x13, other arithmetic  163 us
    all_to_all x1, waiting for transfers between devices, on_device(): lax.all_to_all(spectra[:, send_rows], 'pairs', split_axis=1, concat_axis=...  67 us
    dot_general x12, matrix products, add_block(): jnp.dot(segment, cos_table, preferred_element_type=jnp.float32)  38.8 us
    psum x1, waiting for transfers between devices, on_device(): summed = lax.psum(stacked, 'tm')  33.6 us
    all_gather x1, blocking collectives, on_device(): every_pair = lax.all_gather(pair_stations, 'pairs', axis=0, tiled=True)  22.4 us
    gather x1, local copies, waits for them, and re-layouts, on_device(): spectra[:, send_rows]  12.9 us
    cos x2, other arithmetic, lag_block(): lag_table = jnp.concatenate([jnp.cos(angles), -jnp.sin(angles)], axis=1)  12.9 us
  transfers between devices with their start and end apart: 2, of which 2 were waited for; matrix products, arithmetic and copies ran while one was open for 0% of the time, Pallas kernels for 0%

commit v1 on v0

v1 whole, which is shorter than its diff:
```python
import functools
import math

import jax
import jax.numpy as jnp
import ml_dtypes
import numpy as np
from jax import lax
from jax.experimental import pallas as pl
from jax.experimental.pallas import tpu as pltpu
from jax.sharding import PartitionSpec as P

F = 1536
FLO = 32
LAG = 1024
RADIX = 8
MESH = pl.DeviceIdType.MESH
F32 = jnp.float32
BF16 = jnp.bfloat16


def share_bins(bins_each, tm):
    bins = bins_each // tm
    return bins, -(-bins // 16) * 16


def tables(length, blocks, tm):
    bins_each = F // blocks
    group = blocks // RADIX
    short = length // RADIX
    angles = 2.0 * np.pi * np.arange(length) / length
    cos_of = np.cos(angles).astype(np.float32).astype(ml_dtypes.bfloat16)
    sin_of = np.sin(angles).astype(np.float32).astype(ml_dtypes.bfloat16)
    block_ids = np.arange(blocks)
    first = block_ids // group + RADIX * (block_ids % group) * bins_each
    freqs = FLO + first[:, None] + RADIX * np.arange(bins_each)[None, :]
    phases = freqs[:, :, None] * np.arange(short)[None, None, :] % length
    forward = np.concatenate([cos_of[phases], sin_of[phases]], axis=1)

    bins, half = share_bins(bins_each, tm)
    inside = np.arange(half)
    value = np.arange(tm)[:, None] * bins + np.minimum(inside, bins - 1)[None, :]
    freq = freqs[block_ids[None, :, None], value[:, None, :]].reshape(-1)
    valid = np.broadcast_to(inside < bins, (tm, blocks, half)).reshape(-1)
    lag_phase = freq[None, :] * np.arange(2 * LAG // tm)[:, None] % length
    lag = np.stack([cos_of[lag_phase], -sin_of[lag_phase]])
    lag = np.where(valid, lag, np.zeros((), ml_dtypes.bfloat16))
    return forward.astype(ml_dtypes.bfloat16), lag.astype(ml_dtypes.bfloat16)


def kernel(
    blocks, tm, scale,
    x_hbm, hann, slot_col, ends, tab_hbm, lag_hbm, out,
    x, tab, lag, folded, water, spec_out, spec_in, water_in, ends_in, onehot, white,
    part_out, part_in, pack_out, pack_in, turn,
    local_sem, tab_sem, ends_s, ends_r, spec_s, spec_r, water_s, water_r,
    part_s, part_r, pack_s, pack_r, last_s, last_r,
):
    me, mine = lax.axis_index("pairs"), lax.axis_index("tm")
    bins_each = F // blocks
    group = blocks // RADIX
    length = x.shape[1]
    short = length // RADIX
    bins, half = share_bins(bins_each, tm)
    stations = onehot.shape[1]

    x_copy = pltpu.make_async_copy(x_hbm, x, local_sem.at[0])
    lag_copy = pltpu.make_async_copy(lag_hbm, lag, local_sem.at[1])
    x_copy.start()

    def step_of(i):
        return 1 + (i + blocks // 2 - 1) % (blocks - 1)

    def table_copy(s):
        return pltpu.make_async_copy(tab_hbm.at[(me + s) % blocks], tab.at[s], tab_sem.at[s])

    def start_table(i, c):
        table_copy(step_of(i)).start()
        return c

    lax.fori_loop(0, blocks - 1, start_table, 0)
    table_copy(0).start()
    lag_copy.start()

    def on_pairs(device):
        return {"pairs": device}

    def on_tm(device):
        return {"tm": device}

    barrier = pltpu.get_barrier_semaphore()
    for s in range(1, blocks):
        pl.semaphore_signal(barrier, inc=1, device_id=on_pairs((me + s) % blocks), device_id_type=MESH)
    for s in range(1, tm):
        pl.semaphore_signal(barrier, inc=1, device_id=on_tm((mine + s) % tm), device_id_type=MESH)
    pl.semaphore_wait(barrier, blocks + tm - 2)

    def remote(src, dst, send, recv, device):
        return pltpu.make_async_remote_copy(
            src_ref=src, dst_ref=dst, send_sem=send, recv_sem=recv, device_id=device, device_id_type=MESH
        )

    def ends_copy(s):
        return remote(ends, ends_in.at[me], ends_s.at[s], ends_r.at[s], on_pairs((me + s) % blocks))

    def spec_copy(s):
        return remote(spec_out.at[s], spec_in.at[me], spec_s.at[s], spec_r.at[s], on_pairs((me + s) % blocks))

    def water_copy(s):
        return remote(water, water_in.at[me], water_s.at[s], water_r.at[s], on_pairs((me + s) % blocks))

    def part_copy(s):
        to = (mine + s) % tm
        return remote(part_out.at[to], part_in.at[mine], part_s.at[s], part_r.at[s], on_tm(to))

    def pack_copy(s):
        to = (me + s) % blocks
        return remote(pack_out.at[to], pack_in.at[mine, me], pack_s.at[s], pack_r.at[s], on_pairs(to))

    def last_copy(s):
        return remote(pack_in.at[mine], pack_in.at[mine], last_s.at[s], last_r.at[s], on_tm((mine + s) % tm))

    def each(low, high, act):
        def body(s, c):
            act(s)
            return c
        lax.fori_loop(low, high, body, 0)

    each(1, blocks, lambda s: ends_copy(s).start())
    ends_in[me] = ends[...]

    x_copy.wait()
    root = math.sqrt(0.5)

    def fold(i, c):
        low = pl.ds(pl.multiple_of(i * 16, 16), 16)
        high = pl.ds(pl.multiple_of(128 + i * 16, 16), 16)
        mean = jnp.sum(x[low, :], axis=1, keepdims=True) * (1.0 / length)
        for k in range(short // 128):
            v = []
            for q in range(RADIX):
                cols = slice(q * short + k * 128, q * short + (k + 1) * 128)
                v.append((x[low, cols] - mean) * hann[0:1, cols])
            u = [v[q] + v[q + 4] for q in range(4)]
            d = [v[q] - v[q + 4] for q in range(4)]
            dm, dp = root * (d[1] - d[3]), root * (d[1] + d[3])
            even, odd = u[0] + u[2], u[1] + u[3]
            a2, b2 = u[0] - u[2], u[3] - u[1]
            a1, b1 = d[0] + dm, -d[2] - dp
            a3, b3 = d[0] - dm, d[2] - dp
            zero = jnp.zeros_like(even)
            classes = [
                (even + odd, zero), (a1, b1), (a2, b2), (a3, b3),
                (even - odd, zero), (a3, -b3), (a2, -b2), (a1, -b1),
            ]
            cols = slice(k * 128, (k + 1) * 128)
            for r, (a, b) in enumerate(classes):
                folded[r, low, cols] = a.astype(BF16)
                folded[r, high, cols] = b.astype(BF16)
        return c

    lax.fori_loop(0, 8, fold, 0)
    water[...] = jnp.zeros_like(water)

    def spectrum(s):
        table_copy(s).wait()
        to = (me + s) % blocks
        product = lax.dot_general(
            tab[s], folded[to // group], (((1,), (1,)), ((), ())), preferred_element_type=F32
        )
        re = product[:bins_each, :128] + product[bins_each:, 128:]
        im = product[:bins_each, 128:] - product[bins_each:, :128]
        water[...] += jnp.broadcast_to(jnp.sum(re * re + im * im, axis=0, keepdims=True), water.shape)
        return re.astype(BF16), im.astype(BF16)

    def send_block(i, c):
        s = step_of(i)
        re, im = spectrum(s)
        spec_out[s, :bins_each] = re
        spec_out[s, bins_each:] = im
        spec_copy(s).start()
        return c

    lax.fori_loop(0, blocks - 1, send_block, 0)
    re, im = spectrum(0)
    spec_in[me, :bins_each] = re
    spec_in[me, bins_each:] = im
    water_in[me] = water[...]
    each(1, blocks, lambda s: water_copy(s).start())

    lane = lax.broadcasted_iota(jnp.int32, (1, 128), 1)
    row_ids = lax.broadcasted_iota(jnp.int32, (stations, 256), 0).astype(F32)
    each(1, blocks, lambda s: ends_copy(s).wait())

    def swap(v):
        return pltpu.roll(v, 64, 1)

    def pick(g, c):
        a, b = ends_in[2 * g], ends_in[2 * g + 1]
        left = jnp.where(lane < 64, a, swap(b))[0:1]
        right = jnp.where(lane < 64, swap(a), b)[0:1]
        names = jnp.concatenate([left, right], axis=1)
        slots = jnp.sum(jnp.where(row_ids == names, slot_col[...], 0.0), axis=0, keepdims=True)
        onehot[g] = jnp.where(row_ids == slots, 1.0, 0.0).astype(BF16)
        return c

    lax.fori_loop(0, blocks // 2, pick, 0)

    first_lag = mine * (2 * LAG // tm) - LAG
    inner = lax.broadcasted_iota(jnp.int32, (half, 128), 0).astype(F32)

    def phase_turn(i, c):
        t, block = i // blocks, i % blocks
        base = FLO + block // group + RADIX * ((block % group) * bins_each + t * bins)
        product = (base.astype(F32) + RADIX * inner) * first_lag.astype(F32)
        phase = product - jnp.floor(product * (1.0 / length)) * length
        angle = phase * (2.0 * math.pi / length)
        sine = jnp.sin(angle)
        at = pl.ds(pl.multiple_of(i * half, half), half)
        turn[0, at, :] = jnp.cos(angle)
        turn[1, at, :] = jnp.where(lane < 64, -sine, sine)
        return c

    lax.fori_loop(0, tm * blocks, phase_turn, 0)

    each(1, blocks, lambda s: spec_copy(s).wait())
    each(1, blocks, lambda s: water_copy(s).wait())

    def whiten(src):
        re = spec_in[src, :bins_each].astype(F32)
        im = spec_in[src, bins_each:].astype(F32)
        level = water_in[src][0:1] * (0.1 / F) + 1e-6
        factor = lax.rsqrt(re * re + im * im + level)
        return re * factor, im * factor

    def whiten_two(q, c):
        cols = pl.ds(pl.multiple_of(q * 128, 128), 128)
        one, two = whiten(2 * q), whiten(2 * q + 1)
        for part in range(2):
            first = jnp.where(lane < 64, one[part], swap(two[part]))
            second = jnp.where(lane < 64, swap(one[part]), two[part])
            at = part * bins_each
            white[at:at + bins_each, cols] = first.astype(BF16)
            at += 2 * bins_each
            white[at:at + bins_each, cols] = second.astype(BF16)
        return c

    lax.fori_loop(0, blocks // 2, whiten_two, 0)

    if half > bins:
        part_out[...] = jnp.zeros_like(part_out)

    def cross(g, c):
        got = jnp.dot(white[...], onehot[g], preferred_element_type=F32)
        real = imag = None
        for w in range(2):
            at = 2 * w * bins_each
            lr, rr = got[at:at + bins_each, :128], got[at:at + bins_each, 128:]
            at += bins_each
            li, ri = got[at:at + bins_each, :128], got[at:at + bins_each, 128:]
            re, im = lr * rr + li * ri, li * rr - lr * ri
            real = re if real is None else real + re
            imag = im if imag is None else imag + im
        for t in range(tm):
            part_out[t, g, :bins] = real[t * bins:(t + 1) * bins].astype(BF16)
            part_out[t, g, half:half + bins] = imag[t * bins:(t + 1) * bins].astype(BF16)
        return c

    lax.fori_loop(0, blocks // 2, cross, 0)

    each(1, tm, lambda s: part_copy(s).start())
    part_in[mine] = part_out[mine]
    each(1, tm, lambda s: part_copy(s).wait())

    def pack(g, c):
        total = part_in[0, g].astype(F32)
        for t in range(1, tm):
            total += part_in[t, g].astype(F32)
        top, bottom = total[:half], total[half:]
        pack_out[2 * g] = jnp.where(lane < 64, top, swap(bottom)).astype(BF16)
        pack_out[2 * g + 1] = jnp.where(lane < 64, swap(top), bottom).astype(BF16)
        return c

    lax.fori_loop(0, blocks // 2, pack, 0)
    each(1, blocks, lambda s: pack_copy(s).start())
    pack_in[mine, me] = pack_out[me]
    each(1, blocks, lambda s: pack_copy(s).wait())
    each(1, tm, lambda s: last_copy(s).start())
    lag_copy.wait()
    each(1, tm, lambda s: last_copy(s).wait())

    stacked = pack_in[...].reshape(tm * blocks * half, 128).astype(F32)
    values = (stacked * turn[0] + swap(stacked) * turn[1]).astype(BF16)
    upper = jnp.dot(lag[0], values, preferred_element_type=F32)
    lower = jnp.dot(lag[1], values, preferred_element_type=F32)
    out[...] = ((upper + swap(lower)) * scale)[:, :64]


def on_device(traces, station_slot, pair_stations):
    held, stations_each, length = traces.shape
    stations = station_slot.shape[0]
    blocks, tm = lax.axis_size("pairs"), lax.axis_size("tm")
    pairs_each = pair_stations.shape[0]
    assert held * stations_each == 128 and held == 2 and pairs_each == 64 and blocks % RADIX == 0
    bins_each = F // blocks
    short = length // RADIX
    bins, half = share_bins(bins_each, tm)
    lag_rows = 2 * LAG // tm
    forward, lag = tables(length, blocks, tm)
    times = (np.arange(length, dtype=np.float64) + 0.5) * (2.0 * np.pi / length)
    hann = np.broadcast_to((0.5 - 0.5 * np.cos(times)).astype(np.float32), (8, length))
    ends = jnp.broadcast_to(pair_stations.T.reshape(1, 128).astype(F32), (8, 128))
    slot_col = station_slot.astype(F32).reshape(stations, 1)
    scale = 1.0 / math.sqrt(F * held * tm)
    vmem = pl.BlockSpec(memory_space=pltpu.VMEM)
    anywhere = pl.BlockSpec(memory_space=pl.ANY)
    dma = pltpu.SemaphoreType.DMA
    return pl.pallas_call(
        functools.partial(kernel, blocks, tm, scale),
        out_shape=jax.ShapeDtypeStruct((lag_rows, pairs_each), F32),
        in_specs=[anywhere, vmem, vmem, vmem, anywhere, anywhere],
        out_specs=vmem,
        scratch_shapes=[
            pltpu.VMEM((128, length), F32),
            pltpu.VMEM((blocks, 2 * bins_each, short), BF16),
            pltpu.VMEM((2, lag_rows, tm * blocks * half), BF16),
            pltpu.VMEM((RADIX, 256, short), BF16),
            pltpu.VMEM((8, 128), F32),
            pltpu.VMEM((blocks, 2 * bins_each, 128), BF16),
            pltpu.VMEM((blocks, 2 * bins_each, 128), BF16),
            pltpu.VMEM((blocks, 8, 128), F32),
            pltpu.VMEM((blocks, 8, 128), F32),
            pltpu.VMEM((blocks // 2, stations, 256), BF16),
            pltpu.VMEM((4 * bins_each, stations), BF16),
            pltpu.VMEM((tm, blocks // 2, 2 * half, 128), BF16),
            pltpu.VMEM((tm, blocks // 2, 2 * half, 128), BF16),
            pltpu.VMEM((blocks, half, 128), BF16),
            pltpu.VMEM((tm, blocks, half, 128), BF16),
            pltpu.VMEM((2, tm * blocks * half, 128), F32),
            dma((2,)), dma((blocks,)),
            dma((blocks,)), dma((blocks,)),
            dma((blocks,)), dma((blocks,)),
            dma((blocks,)), dma((blocks,)),
            dma((tm,)), dma((tm,)),
            dma((blocks,)), dma((blocks,)),
            dma((tm,)), dma((tm,)),
        ],
        compiler_params=pltpu.CompilerParams(
            collective_id=0, has_side_effects=True, vmem_limit_bytes=56 * 1024 * 1024
        ),
    )(traces.reshape(128, length), jnp.asarray(hann), slot_col, ends, jnp.asarray(forward), jnp.asarray(lag))


def solution(mesh):
    in_specs = (P("tm", "pairs", None), P(), P("pairs", None))
    out_specs = P("tm", "pairs")
    return jax.shard_map(
        on_device, mesh=mesh, in_specs=in_specs, out_specs=out_specs, check_vma=False
    )
```

time: 405 us -> 53.9 us (0.13)
  other arithmetic: 186 us -> 1.36 us
  waiting for transfers between devices: 101 us -> 0 us
  Pallas kernels: 0 us -> 47.2 us
  matrix products: 44.8 us -> 0 us
  local copies, waits for them, and re-layouts: 31.2 us -> 4.67 us
  blocking collectives: 22.4 us -> 0 us
  between operations: 13.6 us -> 0.01 us
    another operation x14 -> x0, other arithmetic: 165 us -> none
    all_to_all x1 -> x0, waiting for transfers between devices: 67 us -> none  [on_device(): lax.all_to_all(spectra[:, send_rows], 'pairs', split_axis=1, concat_axis=...]
    pallas_call x0 -> x1, Pallas kernels: none -> 47.2 us  [on_device(): pl.pallas_call(functools.partial(kernel, blocks, tm, scale), out_shape=ja...]
    dot_general x14 -> x0, matrix products: 44.8 us -> none  [the longest x12 38.8 us: add_block(): jnp.dot(segment, cos_table, preferred_element_type=jnp.float32)]
    psum x1 -> x0, waiting for transfers between devices: 33.6 us -> none  [on_device(): summed = lax.psum(stacked, 'tm')]
    gather x3 -> x0, local copies, waits for them, and re-layouts: 24.5 us -> none  [the longest x1 12.9 us: on_device(): spectra[:, send_rows]]
    all_gather x1 -> x0, blocking collectives: 22.4 us -> none  [on_device(): every_pair = lax.all_gather(pair_stations, 'pairs', axis=0, tiled=True)]
    cos x2 -> x0, other arithmetic: 12.9 us -> none  [lag_block(): lag_table = jnp.concatenate([jnp.cos(angles), -jnp.sin(angles)], axis=1)]
  transfers between devices with their start and end apart: 2 -> 0, of which waited for: 2 -> 0; matrix products, arithmetic and copies ran while one was open for 0% -> 0% of each run, Pallas kernels for 0% -> 0%
where the time goes in v1:
time: 53.9 us; the launch traced here: 53.3 us
  Pallas kernels  47.2 us (88%)
  local copies, waits for them, and re-layouts  4.67 us (9%)
  other arithmetic  1.36 us (3%)
    pallas_call x1, Pallas kernels, on_device(): pl.pallas_call(functools.partial(kernel, blocks, tm, scale), out_shape=ja...  47.2 us
    pallas_call x1, local copies, waits for them, and re-layouts, on_device(): pl.pallas_call(functools.partial(kernel, blocks, tm, scale), out_shape=ja...  1.72 us
    another operation x1, local copies, waits for them, and re-layouts  1.42 us

profile of v1, /device:TPU:0, one launch (start us, length us, event | category | flops | bytes accessed | tf_op | source)
XLA Modules:
  0.0 53.3 jit_solution(12697456656522981502)
XLA Ops:
  0.0 0.7 %convert_bitcast_fusion = f32[2,64]{1,0:T(2,128)S(1)} fusion(s32[64,2]{0,1:T(2,128)} %param.8), kind=kLoop, calls=%fused_computation | loop fusion | flops 128 | bytes 1024 | tf_op jit(solution)/shard_map/convert_element_type | solution.py:312
  0.7 0.1 convert_element_type.20
  0.8 0.7 %convert_element_type.17 = f32[512]{0:T(512)S(1)} convert(s32[512]{0:T(512)} %param.7) | non-fusion elementwise | flops 512 | bytes 4096 | tf_op jit(solution)/shard_map/convert_element_type | solution.py:313
  1.4 0.6 %broadcast_in_dim.2.ends = f32[8,128]{1,0:T(8,128)} broadcast(f32[128]{0:T(128)S(1)} %convert_element_type.20), dimensions={1} | broadcast | bytes 4608 | tf_op jit(solution)/shard_map/broadcast_in_dim | solution.py:312
  2.0 0.8 %copy.8.slot_col = f32[512,1]{1,0:T(8,128)} copy(f32[512,1]{0,1:T(1,128)S(1)} %bitcast.5) | data formatting | bytes 4096 | tf_op jit(solution)/shard_map/reshape | solution.py:313
  2.9 1.4 %jit_solution_.3.hann = f32[8,6144]{1,0:T(8,128)} broadcast(f32[6144]{0:T(1024)} %constant.6.clone), dimensions={1} | broadcast | bytes 221184 | tf_op jit(solution)
  4.3 47.2 %shard_map.64 = f32[512,64]{1,0:T(8,128)} custom-call(f32[128,6144]{1,0:T(8,128)} %bitcast.4, f32[8,6144]{1,0:T(8,128)} %jit_solution_.3.hann, f32[512,1]{1,0:T(8,128)} %copy.8.slot_col, f32[8,128]{1,0:T(8,128)} %broadcast_in_dim.2.ends, bf16[8,384,768]{2,1,0:T(8,128)(2,1)} %constant.7.clone.tab_hbm, bf16[2,512,1536]{2,1,0:T(8,128)(2,1)} %constant.8.clone.lag_hbm), custom_call_target="tpu_custom_call" | custom-call | tf_op jit(solution)/shard_map/pallas_call | solution.py:318
  51.6 1.7 %copy.9 = f32[512,64]{0,1:T(8,128)} copy(f32[512,64]{1,0:T(8,128)} %shard_map.64) | data formatting | bytes 262144 | tf_op jit(solution)/shard_map/pallas_call | solution.py:318

commit v2 on v1

v2 whole, which is shorter than its diff:
```python
import functools
import math

import jax
import jax.numpy as jnp
import ml_dtypes
import numpy as np
from jax import lax
from jax.experimental import pallas as pl
from jax.experimental.pallas import tpu as pltpu
from jax.sharding import PartitionSpec as P

F = 1536
FLO = 32
LAG = 1024
RADIX = 8
MESH = pl.DeviceIdType.MESH
F32 = jnp.float32
BF16 = jnp.bfloat16


def split(blocks, tm):
    bins_each = F // blocks
    chunks = max(1, bins_each // (16 * tm))
    while bins_each % (chunks * tm):
        chunks -= 1
    bins = bins_each // (chunks * tm)
    return bins_each, chunks, bins, -(-bins // 16) * 16


def tables(length, blocks, tm):
    bins_each, chunks, bins, half = split(blocks, tm)
    group = blocks // RADIX
    short = length // RADIX
    angles = 2.0 * np.pi * np.arange(length) / length
    cos_of = np.cos(angles).astype(np.float32).astype(ml_dtypes.bfloat16)
    sin_of = np.sin(angles).astype(np.float32).astype(ml_dtypes.bfloat16)
    block_ids = np.arange(blocks)
    first = block_ids // group + RADIX * (block_ids % group) * bins_each
    freqs = FLO + first[:, None] + RADIX * np.arange(bins_each)[None, :]
    phases = freqs[:, :, None] * np.arange(short)[None, None, :] % length
    forward = np.concatenate([cos_of[phases], sin_of[phases]], axis=1)

    inside = np.arange(half)
    value = np.arange(chunks * tm)[:, None] * bins + np.minimum(inside, bins - 1)[None, :]
    freq = freqs[block_ids[None, :, None], value[:, None, :]].reshape(chunks, 1, -1)
    valid = np.broadcast_to(inside < bins, (chunks, tm, blocks, half)).reshape(chunks, 1, -1)
    lag_phase = freq * np.arange(2 * LAG // tm)[None, :, None] % length
    zero = np.zeros((), ml_dtypes.bfloat16)
    lag = np.concatenate(
        [np.where(valid, cos_of[lag_phase], zero), np.where(valid, -sin_of[lag_phase], zero)], axis=2
    )
    return forward.astype(ml_dtypes.bfloat16), lag.astype(ml_dtypes.bfloat16)


def kernel(
    blocks, tm, scale,
    x_hbm, hann, slot_row, pairs, tab_hbm, lag_hbm, out,
    x, tab, lag, slot_col, ends, folded, water, spec_out, spec_in, water_in, ends_in, onehot, white,
    part_out, part_in, pack_out, pack_in, turn, total_out,
    local_sem, tab_sem, ends_s, ends_r, spec_s, spec_r, water_s, water_r,
    part_s, part_r, pack_s, pack_r, last_s, last_r,
):
    me, mine = lax.axis_index("pairs"), lax.axis_index("tm")
    bins_each, chunks, bins, half = split(blocks, tm)
    chunk = bins_each // chunks
    group = blocks // RADIX
    length = x.shape[1]
    short = length // RADIX
    stations = onehot.shape[1]

    x_copy = pltpu.make_async_copy(x_hbm, x, local_sem.at[0])
    lag_copy = pltpu.make_async_copy(lag_hbm, lag, local_sem.at[1])
    x_copy.start()

    def step_of(i):
        return 1 + (i + blocks // 2 - 1) % (blocks - 1)

    def table_copy(s):
        return pltpu.make_async_copy(tab_hbm.at[(me + s) % blocks], tab.at[s], tab_sem.at[s])

    def start_table(i, c):
        table_copy(step_of(i)).start()
        return c

    lax.fori_loop(0, blocks - 1, start_table, 0)
    table_copy(0).start()
    lag_copy.start()

    def on_pairs(device):
        return {"pairs": device}

    def on_tm(device):
        return {"tm": device}

    ends[...] = jnp.zeros_like(ends)
    ends[0:1, 0:64] = pairs[0:1, :].astype(F32)
    ends[0:1, 64:128] = pairs[1:2, :].astype(F32)

    barrier = pltpu.get_barrier_semaphore()
    for s in range(1, blocks):
        pl.semaphore_signal(barrier, inc=1, device_id=on_pairs((me + s) % blocks), device_id_type=MESH)
    for s in range(1, tm):
        pl.semaphore_signal(barrier, inc=1, device_id=on_tm((mine + s) % tm), device_id_type=MESH)
    pl.semaphore_wait(barrier, blocks + tm - 2)

    def remote(src, dst, send, recv, device):
        return pltpu.make_async_remote_copy(
            src_ref=src, dst_ref=dst, send_sem=send, recv_sem=recv, device_id=device, device_id_type=MESH
        )

    def ends_copy(s):
        return remote(ends, ends_in.at[me], ends_s.at[s], ends_r.at[s], on_pairs((me + s) % blocks))

    def spec_copy(c, s):
        to = on_pairs((me + s) % blocks)
        return remote(spec_out.at[c, s], spec_in.at[c, me], spec_s.at[c, s], spec_r.at[c, s], to)

    def water_copy(s):
        return remote(water, water_in.at[me], water_s.at[s], water_r.at[s], on_pairs((me + s) % blocks))

    def part_copy(c, s):
        to = (mine + s) % tm
        return remote(part_out.at[c, to], part_in.at[c, mine], part_s.at[c, s], part_r.at[c, s], on_tm(to))

    def pack_copy(c, s):
        to = (me + s) % blocks
        return remote(pack_out.at[c, to], pack_in.at[c, mine, me], pack_s.at[c, s], pack_r.at[c, s], on_pairs(to))

    def last_copy(c, s):
        to = on_tm((mine + s) % tm)
        return remote(pack_in.at[c, mine], pack_in.at[c, mine], last_s.at[c, s], last_r.at[c, s], to)

    def each(low, high, act):
        def body(s, c):
            act(s)
            return c
        lax.fori_loop(low, high, body, 0)

    each(1, blocks, lambda s: ends_copy(s).start())
    ends_in[me] = ends[...]

    x_copy.wait()
    root = math.sqrt(0.5)

    def fold(i, c):
        low = pl.ds(pl.multiple_of(i * 16, 16), 16)
        high = pl.ds(pl.multiple_of(128 + i * 16, 16), 16)
        mean = jnp.sum(x[low, :], axis=1, keepdims=True) * (1.0 / length)
        for k in range(short // 128):
            v = []
            for q in range(RADIX):
                cols = slice(q * short + k * 128, q * short + (k + 1) * 128)
                v.append((x[low, cols] - mean) * hann[q:q + 1, k * 128:(k + 1) * 128])
            u = [v[q] + v[q + 4] for q in range(4)]
            d = [v[q] - v[q + 4] for q in range(4)]
            dm, dp = root * (d[1] - d[3]), root * (d[1] + d[3])
            even, odd = u[0] + u[2], u[1] + u[3]
            a2, b2 = u[0] - u[2], u[3] - u[1]
            a1, b1 = d[0] + dm, -d[2] - dp
            a3, b3 = d[0] - dm, d[2] - dp
            zero = jnp.zeros_like(even)
            classes = [
                (even + odd, zero), (a1, b1), (a2, b2), (a3, b3),
                (even - odd, zero), (a3, -b3), (a2, -b2), (a1, -b1),
            ]
            cols = slice(k * 128, (k + 1) * 128)
            for r, (a, b) in enumerate(classes):
                folded[r, low, cols] = a.astype(BF16)
                folded[r, high, cols] = b.astype(BF16)
        return c

    lax.fori_loop(0, 8, fold, 0)
    water[...] = jnp.zeros_like(water)

    def spectrum(s):
        table_copy(s).wait()
        to = (me + s) % blocks
        product = lax.dot_general(
            tab[s], folded[to // group], (((1,), (1,)), ((), ())), preferred_element_type=F32
        )
        re = product[:bins_each, :128] + product[bins_each:, 128:]
        im = product[:bins_each, 128:] - product[bins_each:, :128]
        water[...] += jnp.broadcast_to(jnp.sum(re * re + im * im, axis=0, keepdims=True), water.shape)
        return re.astype(BF16), im.astype(BF16)

    def send_block(i, c):
        s = step_of(i)
        re, im = spectrum(s)
        for part in range(chunks):
            spec_out[part, s, :chunk] = re[part * chunk:(part + 1) * chunk]
            spec_out[part, s, chunk:] = im[part * chunk:(part + 1) * chunk]
        spec_copy(0, s).start()
        return c

    lax.fori_loop(0, blocks - 1, send_block, 0)
    re, im = spectrum(0)
    for part in range(chunks):
        spec_in[part, me, :chunk] = re[part * chunk:(part + 1) * chunk]
        spec_in[part, me, chunk:] = im[part * chunk:(part + 1) * chunk]
    water_in[me] = water[...]
    each(1, blocks, lambda s: water_copy(s).start())
    for part in range(1, chunks):
        each(0, blocks - 1, lambda i: spec_copy(part, step_of(i)).start())

    for k in range(stations // 128):
        cols = slice(k * 128, (k + 1) * 128)
        slot_col[cols, :] = jnp.broadcast_to(slot_row[0:1, cols].astype(F32), (128, 128)).T
    lane = lax.broadcasted_iota(jnp.int32, (1, 128), 1)
    row_ids = lax.broadcasted_iota(jnp.int32, (stations, 256), 0).astype(F32)
    each(1, blocks, lambda s: ends_copy(s).wait())

    def swap(v):
        return pltpu.roll(v, 64, 1)

    def pick(g, c):
        a, b = ends_in[2 * g], ends_in[2 * g + 1]
        left = jnp.where(lane < 64, a, swap(b))[0:1]
        right = jnp.where(lane < 64, swap(a), b)[0:1]
        names = jnp.concatenate([left, right], axis=1)
        slots = jnp.concatenate([slot_col[...], slot_col[...]], axis=1)
        slots = jnp.sum(jnp.where(row_ids == names, slots, 0.0), axis=0, keepdims=True)
        onehot[g] = jnp.where(row_ids == slots, 1.0, 0.0).astype(BF16)
        return c

    lax.fori_loop(0, blocks // 2, pick, 0)

    first_lag = mine * (2 * LAG // tm) - LAG
    inner = lax.broadcasted_iota(jnp.int32, (half, 128), 0).astype(F32)

    def phase_turn(i, c):
        share, block = i // blocks, i % blocks
        base = FLO + block // group + RADIX * ((block % group) * bins_each + share * bins)
        product = (base.astype(F32) + RADIX * inner) * first_lag.astype(F32)
        phase = product - jnp.floor(product * (1.0 / length)) * length
        angle = phase * (2.0 * math.pi / length)
        sine = jnp.sin(angle)
        at = pl.ds(pl.multiple_of(i * half, half), half)
        turn[0, at, :] = jnp.cos(angle)
        turn[1, at, :] = jnp.where(lane < 64, -sine, sine)
        return c

    if half > bins:
        part_out[...] = jnp.zeros_like(part_out)

    def cross_chunk(part):
        def whiten(src):
            re = spec_in[part, src, :chunk].astype(F32)
            im = spec_in[part, src, chunk:].astype(F32)
            level = water_in[src][0:1] * (0.1 / F) + 1e-6
            factor = lax.rsqrt(re * re + im * im + level)
            return re * factor, im * factor

        def whiten_two(q, c):
            cols = pl.ds(pl.multiple_of(q * 128, 128), 128)
            one, two = whiten(2 * q), whiten(2 * q + 1)
            for k in range(2):
                first = jnp.where(lane < 64, one[k], swap(two[k]))
                second = jnp.where(lane < 64, swap(one[k]), two[k])
                at = k * chunk
                white[at:at + chunk, cols] = first.astype(BF16)
                at += 2 * chunk
                white[at:at + chunk, cols] = second.astype(BF16)
            return c

        lax.fori_loop(0, blocks // 2, whiten_two, 0)

        def cross(g, c):
            got = jnp.dot(white[...], onehot[g], preferred_element_type=F32)
            real = imag = None
            for w in range(2):
                at = 2 * w * chunk
                lr, rr = got[at:at + chunk, :128], got[at:at + chunk, 128:]
                at += chunk
                li, ri = got[at:at + chunk, :128], got[at:at + chunk, 128:]
                re, im = lr * rr + li * ri, li * rr - lr * ri
                real = re if real is None else real + re
                imag = im if imag is None else imag + im
            for t in range(tm):
                rows = slice(t * bins, (t + 1) * bins)
                part_out[part, t, g, :bins] = real[rows].astype(BF16)
                part_out[part, t, g, half:half + bins] = imag[rows].astype(BF16)
            return c

        lax.fori_loop(0, blocks // 2, cross, 0)
        each(1, tm, lambda s: part_copy(part, s).start())
        part_in[part, mine] = part_out[part, mine]

    def pack_chunk(part):
        each(1, tm, lambda s: part_copy(part, s).wait())

        def pack(g, c):
            total = part_in[part, 0, g].astype(F32)
            for t in range(1, tm):
                total += part_in[part, t, g].astype(F32)
            top, bottom = total[:half], total[half:]
            pack_out[part, 2 * g] = jnp.where(lane < 64, top, swap(bottom)).astype(BF16)
            pack_out[part, 2 * g + 1] = jnp.where(lane < 64, swap(top), bottom).astype(BF16)
            return c

        lax.fori_loop(0, blocks // 2, pack, 0)
        each(1, blocks, lambda s: pack_copy(part, s).start())
        pack_in[part, mine, me] = pack_out[part, me]

    def share_chunk(part):
        each(1, blocks, lambda s: pack_copy(part, s).wait())
        each(1, tm, lambda s: last_copy(part, s).start())

    def lag_chunk(part):
        each(1, tm, lambda s: last_copy(part, s).wait())
        count = tm * blocks * half
        at = slice(part * count, (part + 1) * count)
        stacked = pack_in[part].reshape(count, 128).astype(F32)
        turned = stacked * turn[0, at, :] + swap(stacked) * turn[1, at, :]
        values = jnp.concatenate([turned, swap(turned)], axis=0).astype(BF16)
        product = jnp.dot(lag[part], values, preferred_element_type=F32)
        total_out[...] = product if part == 0 else total_out[...] + product

    each(1, blocks, lambda s: water_copy(s).wait())
    for part in range(chunks):
        each(1, blocks, lambda s: spec_copy(part, s).wait())
        cross_chunk(part)
        if part == 0:
            lax.fori_loop(0, chunks * tm * blocks, phase_turn, 0)
            lag_copy.wait()
        else:
            share_chunk(part - 1)
        pack_chunk(part)
    for part in range(chunks - 1):
        lag_chunk(part)
    share_chunk(chunks - 1)
    lag_chunk(chunks - 1)
    out[...] = (total_out[...] * scale).T[:64]


def on_device(traces, station_slot, pair_stations):
    held, stations_each, length = traces.shape
    stations = station_slot.shape[0]
    blocks, tm = lax.axis_size("pairs"), lax.axis_size("tm")
    pairs_each = pair_stations.shape[0]
    assert held * stations_each == 128 and held == 2 and pairs_each == 64 and blocks % RADIX == 0
    bins_each, chunks, bins, half = split(blocks, tm)
    short = length // RADIX
    values = tm * blocks * half
    lag_rows = 2 * LAG // tm
    forward, lag = tables(length, blocks, tm)
    times = (np.arange(length, dtype=np.float64) + 0.5) * (2.0 * np.pi / length)
    hann = (0.5 - 0.5 * np.cos(times)).astype(np.float32).reshape(RADIX, short)
    scale = 1.0 / math.sqrt(F * held * tm)
    vmem = pl.BlockSpec(memory_space=pltpu.VMEM)
    anywhere = pl.BlockSpec(memory_space=pl.ANY)
    dma = pltpu.SemaphoreType.DMA
    result = pl.pallas_call(
        functools.partial(kernel, blocks, tm, scale),
        out_shape=jax.ShapeDtypeStruct((pairs_each, lag_rows), F32),
        in_specs=[anywhere, vmem, vmem, vmem, anywhere, anywhere],
        out_specs=vmem,
        scratch_shapes=[
            pltpu.VMEM((128, length), F32),
            pltpu.VMEM((blocks, 2 * bins_each, short), BF16),
            pltpu.VMEM((chunks, lag_rows, 2 * values), BF16),
            pltpu.VMEM((stations, 128), F32),
            pltpu.VMEM((8, 128), F32),
            pltpu.VMEM((RADIX, 256, short), BF16),
            pltpu.VMEM((8, 128), F32),
            pltpu.VMEM((chunks, blocks, 2 * bins_each // chunks, 128), BF16),
            pltpu.VMEM((chunks, blocks, 2 * bins_each // chunks, 128), BF16),
            pltpu.VMEM((blocks, 8, 128), F32),
            pltpu.VMEM((blocks, 8, 128), F32),
            pltpu.VMEM((blocks // 2, stations, 256), BF16),
            pltpu.VMEM((4 * bins_each // chunks, stations), BF16),
            pltpu.VMEM((chunks, tm, blocks // 2, 2 * half, 128), BF16),
            pltpu.VMEM((chunks, tm, blocks // 2, 2 * half, 128), BF16),
            pltpu.VMEM((chunks, blocks, half, 128), BF16),
            pltpu.VMEM((chunks, tm, blocks, half, 128), BF16),
            pltpu.VMEM((2, chunks * values, 128), F32),
            pltpu.VMEM((lag_rows, 128), F32),
            dma((2,)), dma((blocks,)),
            dma((blocks,)), dma((blocks,)),
            dma((chunks, blocks)), dma((chunks, blocks)),
            dma((blocks,)), dma((blocks,)),
            dma((chunks, tm)), dma((chunks, tm)),
            dma((chunks, blocks)), dma((chunks, blocks)),
            dma((chunks, tm)), dma((chunks, tm)),
        ],
        compiler_params=pltpu.CompilerParams(
            collective_id=0, has_side_effects=True, vmem_limit_bytes=56 * 1024 * 1024
        ),
    )(
        traces.reshape(128, length), jnp.asarray(hann), station_slot.reshape(1, stations),
        pair_stations.T, jnp.asarray(forward), jnp.asarray(lag),
    )
    return result.T


def solution(mesh):
    in_specs = (P("tm", "pairs", None), P(), P("pairs", None))
    out_specs = P("tm", "pairs")
    return jax.shard_map(
        on_device, mesh=mesh, in_specs=in_specs, out_specs=out_specs, check_vma=False
    )
```

time: 53.9 us -> 52.1 us (0.967)
  Pallas kernels: 47.2 us -> 50.4 us
  local copies, waits for them, and re-layouts: 4.67 us -> 1.57 us
  other arithmetic: 1.36 us -> 0 us
    pallas_call x1, Pallas kernels: 47.2 us -> 50.4 us  [on_device(): pl.pallas_call(functools.partial(kernel, blocks, tm, scale), out_shape=ja...]
    pallas_call x1 -> x0, local copies, waits for them, and re-layouts: 1.72 us -> none  [on_device(): pl.pallas_call(functools.partial(kernel, blocks, tm, scale), out_shape=ja...]
    unnamed x0 -> x1, local copies, waits for them, and re-layouts: none -> 1.57 us
    another operation x1 -> x0, local copies, waits for them, and re-layouts: 1.42 us -> none
    convert_element_type x2 -> x0, other arithmetic: 1.36 us -> none  [the longest x1 0.68 us: on_device(): slot_col = station_slot.astype(F32).reshape(stations, 1)]
    reshape x1 -> x0, local copies, waits for them, and re-layouts: 0.85 us -> none  [on_device(): slot_col = station_slot.astype(F32).reshape(stations, 1)]
    broadcast_in_dim x1 -> x0, local copies, waits for them, and re-layouts: 0.59 us -> none  [on_device(): jnp.broadcast_to(pair_stations.T.reshape(1, 128).astype(F32), (8, 128))]
where the time goes in v2:
time: 52.1 us; the launch traced here: 51.9 us
  Pallas kernels  50.4 us (97%)
  local copies, waits for them, and re-layouts  1.57 us (3%)
    pallas_call x1, Pallas kernels, on_device(): pl.pallas_call(functools.partial(kernel, blocks, tm, scale), out_shape=ja...  50.4 us
    unnamed x1, local copies, waits for them, and re-layouts  1.57 us

profile of v2, /device:TPU:0, one launch (start us, length us, event | category | flops | bytes accessed | tf_op | source)
XLA Modules:
  0.0 51.9 jit_solution(11285825250938154385)
XLA Ops:
  0.0 50.4 %shard_map.64 = f32[64,512]{1,0:T(8,128)} custom-call(f32[128,6144]{1,0:T(8,128)} %bitcast.4, f32[8,768]{1,0:T(8,128)} %constant.6.clone.hann, s32[1,512]{1,0:T(1,128)} %bitcast.6, s32[2,64]{1,0:T(2,128)} %bitcast.7, bf16[8,384,768]{2,1,0:T(8,128)(2,1)} %constant.7.clone.tab_hbm, bf16[3,512,1024]{2,1,0:T(8,128)(2,1)} %constant.8.clone.lag_hbm), custom_call_target="tpu_custom_call" | custom-call | tf_op jit(solution)/shard_map/pallas_call | solution.py:353
  50.4 1.6 %copy.8 = f32[512,64]{0,1:T(8,128)} copy(f32[512,64]{0,1:T(8,128)} %bitcast.5) | data formatting | bytes 262144

commit v3 on v2

--- a/solution.py
+++ b/solution.py
@@ -50,12 +50,17 @@
     lag = np.concatenate(
         [np.where(valid, cos_of[lag_phase], zero), np.where(valid, -sin_of[lag_phase], zero)], axis=2
     )
-    return forward.astype(ml_dtypes.bfloat16), lag.astype(ml_dtypes.bfloat16)
+    first_lag = np.arange(tm) * (2 * LAG // tm) - LAG
+    turn_angle = 2.0 * np.pi / length * (freq.reshape(1, -1) * first_lag[:, None] % length)
+    cosine, sine = np.cos(turn_angle), np.sin(turn_angle)
+    turn = np.stack([np.stack([cosine, cosine], axis=2), np.stack([-sine, sine], axis=2)], axis=1)
+    turn = np.repeat(turn.astype(np.float32), 64, axis=3)
+    return forward.astype(ml_dtypes.bfloat16), lag.astype(ml_dtypes.bfloat16), turn
 
 
 def kernel(
     blocks, tm, scale,
-    x_hbm, hann, slot_row, pairs, tab_hbm, lag_hbm, out,
+    x_hbm, hann, slot_row, pairs, tab_hbm, lag_hbm, turn_hbm, out,
     x, tab, lag, slot_col, ends, folded, water, spec_out, spec_in, water_in, ends_in, onehot, white,
     part_out, part_in, pack_out, pack_in, turn, total_out,
     local_sem, tab_sem, ends_s, ends_r, spec_s, spec_r, water_s, water_r,
@@ -71,6 +76,7 @@
 
     x_copy = pltpu.make_async_copy(x_hbm, x, local_sem.at[0])
     lag_copy = pltpu.make_async_copy(lag_hbm, lag, local_sem.at[1])
+    turn_copy = pltpu.make_async_copy(turn_hbm.at[mine], turn, local_sem.at[2])
     x_copy.start()
 
     def step_of(i):
@@ -86,6 +92,7 @@
     lax.fori_loop(0, blocks - 1, start_table, 0)
     table_copy(0).start()
     lag_copy.start()
+    turn_copy.start()
 
     def on_pairs(device):
         return {"pairs": device}
@@ -102,8 +109,6 @@
         pl.semaphore_signal(barrier, inc=1, device_id=on_pairs((me + s) % blocks), device_id_type=MESH)
     for s in range(1, tm):
         pl.semaphore_signal(barrier, inc=1, device_id=on_tm((mine + s) % tm), device_id_type=MESH)
-    pl.semaphore_wait(barrier, blocks + tm - 2)
-
     def remote(src, dst, send, recv, device):
         return pltpu.make_async_remote_copy(
             src_ref=src, dst_ref=dst, send_sem=send, recv_sem=recv, device_id=device, device_id_type=MESH
@@ -136,9 +141,6 @@
             act(s)
             return c
         lax.fori_loop(low, high, body, 0)
-
-    each(1, blocks, lambda s: ends_copy(s).start())
-    ends_in[me] = ends[...]
 
     x_copy.wait()
     root = math.sqrt(0.5)
@@ -173,6 +175,10 @@
     lax.fori_loop(0, 8, fold, 0)
     water[...] = jnp.zeros_like(water)
 
+    pl.semaphore_wait(barrier, blocks + tm - 2)
+    each(1, blocks, lambda s: ends_copy(s).start())
+    ends_in[me] = ends[...]
+
     def spectrum(s):
         table_copy(s).wait()
         to = (me + s) % blocks
@@ -200,8 +206,15 @@
         spec_in[part, me, chunk:] = im[part * chunk:(part + 1) * chunk]
     water_in[me] = water[...]
     each(1, blocks, lambda s: water_copy(s).start())
-    for part in range(1, chunks):
-        each(0, blocks - 1, lambda i: spec_copy(part, step_of(i)).start())
+
+    def send_next(part):
+        def body(i, c):
+            s = step_of(i)
+            spec_copy(part, s).wait_send()
+            if part + 1 < chunks:
+                spec_copy(part + 1, s).start()
+            return c
+        lax.fori_loop(0, blocks - 1, body, 0)
 
     for k in range(stations // 128):
         cols = slice(k * 128, (k + 1) * 128)
@@ -224,21 +237,6 @@
         return c
 
     lax.fori_loop(0, blocks // 2, pick, 0)
-
-    first_lag = mine * (2 * LAG // tm) - LAG
-    inner = lax.broadcasted_iota(jnp.int32, (half, 128), 0).astype(F32)
-
-    def phase_turn(i, c):
-        share, block = i // blocks, i % blocks
-        base = FLO + block // group + RADIX * ((block % group) * bins_each + share * bins)
-        product = (base.astype(F32) + RADIX * inner) * first_lag.astype(F32)
-        phase = product - jnp.floor(product * (1.0 / length)) * length
-        angle = phase * (2.0 * math.pi / length)
-        sine = jnp.sin(angle)
-        at = pl.ds(pl.multiple_of(i * half, half), half)
-        turn[0, at, :] = jnp.cos(angle)
-        turn[1, at, :] = jnp.where(lane < 64, -sine, sine)
-        return c
 
     if half > bins:
         part_out[...] = jnp.zeros_like(part_out)
@@ -316,16 +314,19 @@
         product = jnp.dot(lag[part], values, preferred_element_type=F32)
         total_out[...] = product if part == 0 else total_out[...] + product
 
+    send_next(0)
     each(1, blocks, lambda s: water_copy(s).wait())
     for part in range(chunks):
-        each(1, blocks, lambda s: spec_copy(part, s).wait())
+        each(1, blocks, lambda s: spec_copy(part, s).wait_recv())
         cross_chunk(part)
         if part == 0:
-            lax.fori_loop(0, chunks * tm * blocks, phase_turn, 0)
             lag_copy.wait()
+            turn_copy.wait()
         else:
             share_chunk(part - 1)
         pack_chunk(part)
+        if part + 1 < chunks:
+            send_next(part + 1)
     for part in range(chunks - 1):
         lag_chunk(part)
     share_chunk(chunks - 1)
@@ -343,7 +344,7 @@
     short = length // RADIX
     values = tm * blocks * half
     lag_rows = 2 * LAG // tm
-    forward, lag = tables(length, blocks, tm)
+    forward, lag, turn = tables(length, blocks, tm)
     times = (np.arange(length, dtype=np.float64) + 0.5) * (2.0 * np.pi / length)
     hann = (0.5 - 0.5 * np.cos(times)).astype(np.float32).reshape(RADIX, short)
     scale = 1.0 / math.sqrt(F * held * tm)
@@ -353,7 +354,7 @@
     result = pl.pallas_call(
         functools.partial(kernel, blocks, tm, scale),
         out_shape=jax.ShapeDtypeStruct((pairs_each, lag_rows), F32),
-        in_specs=[anywhere, vmem, vmem, vmem, anywhere, anywhere],
+        in_specs=[anywhere, vmem, vmem, vmem, anywhere, anywhere, anywhere],
         out_specs=vmem,
         scratch_shapes=[
             pltpu.VMEM((128, length), F32),
@@ -375,7 +376,7 @@
             pltpu.VMEM((chunks, tm, blocks, half, 128), BF16),
             pltpu.VMEM((2, chunks * values, 128), F32),
             pltpu.VMEM((lag_rows, 128), F32),
-            dma((2,)), dma((blocks,)),
+            dma((3,)), dma((blocks,)),
             dma((blocks,)), dma((blocks,)),
             dma((chunks, blocks)), dma((chunks, blocks)),
             dma((blocks,)), dma((blocks,)),
@@ -388,7 +389,7 @@
         ),
     )(
         traces.reshape(128, length), jnp.asarray(hann), station_slot.reshape(1, stations),
-        pair_stations.T, jnp.asarray(forward), jnp.asarray(lag),
+        pair_stations.T, jnp.asarray(forward), jnp.asarray(lag), jnp.asarray(turn),
     )
     return result.T
 

time: 52.1 us -> 50 us (0.960)
  Pallas kernels: 50.4 us -> 48.3 us
    pallas_call x1, Pallas kernels: 50.4 us -> 48.3 us  [on_device(): pl.pallas_call(functools.partial(kernel, blocks, tm, scale), out_shape=ja...]
where the time goes in v3:
time: 50 us; the launch traced here: 49.8 us
  Pallas kernels  48.3 us (97%)
  local copies, waits for them, and re-layouts  1.57 us (3%)
    pallas_call x1, Pallas kernels, on_device(): pl.pallas_call(functools.partial(kernel, blocks, tm, scale), out_shape=ja...  48.3 us
    unnamed x1, local copies, waits for them, and re-layouts  1.57 us

profile of v3, /device:TPU:0, one launch (start us, length us, event | category | flops | bytes accessed | tf_op | source)
XLA Modules:
  0.0 49.8 jit_solution(1128854040605978498)
XLA Ops:
  0.0 48.3 %shard_map.73 = f32[64,512]{1,0:T(8,128)} custom-call(f32[128,6144]{1,0:T(8,128)} %bitcast.4, f32[8,768]{1,0:T(8,128)} %constant.8.clone.hann, s32[1,512]{1,0:T(1,128)} %bitcast.6, s32[2,64]{1,0:T(2,128)} %bitcast.7, bf16[8,384,768]{2,1,0:T(8,128)(2,1)} %constant.9.clone.tab_hbm, bf16[3,512,1024]{2,1,0:T(8,128)(2,1)} %constant.10.clone.lag_hbm, ...), custom_call_target="tpu_custom_call" | custom-call | tf_op jit(solution)/shard_map/pallas_call | solution.py:354
  48.3 1.6 %copy.9 = f32[512,64]{0,1:T(8,128)} copy(f32[512,64]{0,1:T(8,128)} %bitcast.5) | data formatting | bytes 262144

commit v4 on v3

--- a/solution.py
+++ b/solution.py
@@ -59,11 +59,11 @@
 
 
 def kernel(
-    blocks, tm, scale,
-    x_hbm, hann, slot_row, pairs, tab_hbm, lag_hbm, turn_hbm, out,
-    x, tab, lag, slot_col, ends, folded, water, spec_out, spec_in, water_in, ends_in, onehot, white,
+    blocks, tm,
+    x_hbm, hann_hbm, slot_hbm, pairs_hbm, tab_hbm, lag_hbm, turn_hbm, out,
+    x, hann, slot_row, pairs, tab, lag, slot_col, ends, folded, water, spec_out, spec_in, water_in, ends_in, onehot, white,
     part_out, part_in, pack_out, pack_in, turn, total_out,
-    local_sem, tab_sem, ends_s, ends_r, spec_s, spec_r, water_s, water_r,
+    local_sem, x_sem, tab_sem, ends_s, ends_r, spec_s, spec_r, water_s, water_r,
     part_s, part_r, pack_s, pack_r, last_s, last_r,
 ):
     me, mine = lax.axis_index("pairs"), lax.axis_index("tm")
@@ -74,10 +74,20 @@
     short = length // RADIX
     stations = onehot.shape[1]
 
-    x_copy = pltpu.make_async_copy(x_hbm, x, local_sem.at[0])
-    lag_copy = pltpu.make_async_copy(lag_hbm, lag, local_sem.at[1])
-    turn_copy = pltpu.make_async_copy(turn_hbm.at[mine], turn, local_sem.at[2])
-    x_copy.start()
+    lag_copy = pltpu.make_async_copy(lag_hbm, lag, local_sem.at[0])
+    turn_copy = pltpu.make_async_copy(turn_hbm.at[mine], turn, local_sem.at[1])
+    hann_copy = pltpu.make_async_copy(hann_hbm, hann, local_sem.at[2])
+    slot_copy = pltpu.make_async_copy(slot_hbm, slot_row, local_sem.at[3])
+    pairs_copy = pltpu.make_async_copy(pairs_hbm, pairs, local_sem.at[4])
+
+    def x_copy(i):
+        at = pl.ds(pl.multiple_of(i * 16, 16), 16)
+        return pltpu.make_async_copy(x_hbm.at[at], x.at[at], x_sem.at[i])
+
+    hann_copy.start()
+    x_copy(0).start()
+    pairs_copy.start()
+    slot_copy.start()
 
     def step_of(i):
         return 1 + (i + blocks // 2 - 1) % (blocks - 1)
@@ -85,30 +95,20 @@
     def table_copy(s):
         return pltpu.make_async_copy(tab_hbm.at[(me + s) % blocks], tab.at[s], tab_sem.at[s])
 
-    def start_table(i, c):
-        table_copy(step_of(i)).start()
-        return c
-
-    lax.fori_loop(0, blocks - 1, start_table, 0)
-    table_copy(0).start()
-    lag_copy.start()
-    turn_copy.start()
-
     def on_pairs(device):
         return {"pairs": device}
 
     def on_tm(device):
         return {"tm": device}
-
-    ends[...] = jnp.zeros_like(ends)
-    ends[0:1, 0:64] = pairs[0:1, :].astype(F32)
-    ends[0:1, 64:128] = pairs[1:2, :].astype(F32)
 
     barrier = pltpu.get_barrier_semaphore()
     for s in range(1, blocks):
         pl.semaphore_signal(barrier, inc=1, device_id=on_pairs((me + s) % blocks), device_id_type=MESH)
     for s in range(1, tm):
         pl.semaphore_signal(barrier, inc=1, device_id=on_tm((mine + s) % tm), device_id_type=MESH)
+    for i in range(1, 8):
+        x_copy(i).start()
+
     def remote(src, dst, send, recv, device):
         return pltpu.make_async_remote_copy(
             src_ref=src, dst_ref=dst, send_sem=send, recv_sem=recv, device_id=device, device_id_type=MESH
@@ -142,12 +142,16 @@
             return c
         lax.fori_loop(low, high, body, 0)
 
-    x_copy.wait()
+    hann_copy.wait()
     root = math.sqrt(0.5)
 
     def fold(i, c):
         low = pl.ds(pl.multiple_of(i * 16, 16), 16)
         high = pl.ds(pl.multiple_of(128 + i * 16, 16), 16)
+        x_copy(i).wait()
+        for k in range(group):
+            at = i * group + k
+            table_copy(jnp.where(at < blocks - 1, step_of(at), 0)).start()
         mean = jnp.sum(x[low, :], axis=1, keepdims=True) * (1.0 / length)
         for k in range(short // 128):
             v = []
@@ -176,6 +180,10 @@
     water[...] = jnp.zeros_like(water)
 
     pl.semaphore_wait(barrier, blocks + tm - 2)
+    pairs_copy.wait()
+    ends[...] = jnp.zeros_like(ends)
+    ends[0:1, 0:64] = pairs[0:1, :].astype(F32)
+    ends[0:1, 64:128] = pairs[1:2, :].astype(F32)
     each(1, blocks, lambda s: ends_copy(s).start())
     ends_in[me] = ends[...]
 
@@ -216,6 +224,7 @@
             return c
         lax.fori_loop(0, blocks - 1, body, 0)
 
+    slot_copy.wait()
     for k in range(stations // 128):
         cols = slice(k * 128, (k + 1) * 128)
         slot_col[cols, :] = jnp.broadcast_to(slot_row[0:1, cols].astype(F32), (128, 128)).T
@@ -314,24 +323,26 @@
         product = jnp.dot(lag[part], values, preferred_element_type=F32)
         total_out[...] = product if part == 0 else total_out[...] + product
 
+    lag_copy.start()
+    turn_copy.start()
     send_next(0)
     each(1, blocks, lambda s: water_copy(s).wait())
     for part in range(chunks):
         each(1, blocks, lambda s: spec_copy(part, s).wait_recv())
         cross_chunk(part)
+        if part + 1 < chunks:
+            send_next(part + 1)
         if part == 0:
             lag_copy.wait()
             turn_copy.wait()
         else:
             share_chunk(part - 1)
         pack_chunk(part)
-        if part + 1 < chunks:
-            send_next(part + 1)
     for part in range(chunks - 1):
         lag_chunk(part)
     share_chunk(chunks - 1)
     lag_chunk(chunks - 1)
-    out[...] = (total_out[...] * scale).T[:64]
+    out[...] = total_out[...].T[:64]
 
 
 def on_device(traces, station_slot, pair_stations):
@@ -352,12 +363,15 @@
     anywhere = pl.BlockSpec(memory_space=pl.ANY)
     dma = pltpu.SemaphoreType.DMA
     result = pl.pallas_call(
-        functools.partial(kernel, blocks, tm, scale),
+        functools.partial(kernel, blocks, tm),
         out_shape=jax.ShapeDtypeStruct((pairs_each, lag_rows), F32),
-        in_specs=[anywhere, vmem, vmem, vmem, anywhere, anywhere, anywhere],
+        in_specs=[anywhere, anywhere, anywhere, anywhere, anywhere, anywhere, anywhere],
         out_specs=vmem,
         scratch_shapes=[
             pltpu.VMEM((128, length), F32),
+            pltpu.VMEM((RADIX, short), F32),
+            pltpu.VMEM((1, stations), jnp.int32),
+            pltpu.VMEM((2, pairs_each), jnp.int32),
             pltpu.VMEM((blocks, 2 * bins_each, short), BF16),
             pltpu.VMEM((chunks, lag_rows, 2 * values), BF16),
             pltpu.VMEM((stations, 128), F32),
@@ -376,7 +390,7 @@
             pltpu.VMEM((chunks, tm, blocks, half, 128), BF16),
             pltpu.VMEM((2, chunks * values, 128), F32),
             pltpu.VMEM((lag_rows, 128), F32),
-            dma((3,)), dma((blocks,)),
+            dma((5,)), dma((8,)), dma((blocks,)),
             dma((blocks,)), dma((blocks,)),
             dma((chunks, blocks)), dma((chunks, blocks)),
             dma((blocks,)), dma((blocks,)),
@@ -391,7 +405,7 @@
         traces.reshape(128, length), jnp.asarray(hann), station_slot.reshape(1, stations),
         pair_stations.T, jnp.asarray(forward), jnp.asarray(lag), jnp.asarray(turn),
     )
-    return result.T
+    return result.T * scale
 
 
 def solution(mesh):

time: 50 us -> 45.2 us (0.904)
  Pallas kernels: 48.3 us -> 43.5 us
  other arithmetic: 0 us -> 1.57 us
  local copies, waits for them, and re-layouts: 1.57 us -> 0 us
    pallas_call x1, Pallas kernels: 48.3 us -> 43.5 us  [on_device(): pl.pallas_call(functools.partial(kernel, blocks, tm), out_shape=jax.Shape...]
    mul x0 -> x1, other arithmetic: none -> 1.57 us  [on_device(): return result.T * scale]
    unnamed x1 -> x0, local copies, waits for them, and re-layouts: 1.57 us -> none
where the time goes in v4:
time: 45.2 us; the launch traced here: 45.1 us
  Pallas kernels  43.5 us (96%)
  other arithmetic  1.57 us (3%)
    pallas_call x1, Pallas kernels, on_device(): pl.pallas_call(functools.partial(kernel, blocks, tm), out_shape=jax.Shape...  43.5 us
    mul x1, other arithmetic, on_device(): return result.T * scale  1.57 us

profile of v4, /device:TPU:0, one launch (start us, length us, event | category | flops | bytes accessed | tf_op | source)
XLA Modules:
  0.0 45.1 jit_solution(15872678171854630339)
XLA Ops:
  0.0 43.5 %shard_map.73 = f32[64,512]{1,0:T(8,128)} custom-call(f32[128,6144]{1,0:T(8,128)} %bitcast.5, f32[8,768]{1,0:T(8,128)} %constant.10.clone.hann_hbm, s32[1,512]{1,0:T(1,128)} %bitcast.6, s32[2,64]{1,0:T(2,128)} %bitcast.7, bf16[8,384,768]{2,1,0:T(8,128)(2,1)} %constant.11.clone.tab_hbm, bf16[3,512,1024]{2,1,0:T(8,128)(2,1)} %constant.12.clone.lag_hbm, ...), custom_call_target="tpu_custom_call" | custom-call | tf_op jit(solution)/shard_map/pallas_call | solution.py:365
  43.5 1.6 %multiply_bitcast_fusion = f32[512,64]{0,1:T(8,128)} fusion(f32[64,512]{1,0:T(8,128)} %shard_map.73), kind=kLoop, calls=%fused_computation | loop fusion | flops 32768 | bytes 262144 | tf_op jit(solution)/shard_map/mul | solution.py:408

commit v5 on v4

--- a/solution.py
+++ b/solution.py
@@ -14,6 +14,7 @@
 FLO = 32
 LAG = 1024
 RADIX = 8
+CORES = 2
 MESH = pl.DeviceIdType.MESH
 F32 = jnp.float32
 BF16 = jnp.bfloat16
@@ -65,10 +66,12 @@
     part_out, part_in, pack_out, pack_in, turn, total_out,
     local_sem, x_sem, tab_sem, ends_s, ends_r, spec_s, spec_r, water_s, water_r,
     part_s, part_r, pack_s, pack_r, last_s, last_r,
+    wide_s, wide_r, core_s, core_r,
 ):
     me, mine = lax.axis_index("pairs"), lax.axis_index("tm")
     bins_each, chunks, bins, half = split(blocks, tm)
     chunk = bins_each // chunks
+    chips = tm // CORES
     group = blocks // RADIX
     length = x.shape[1]
     short = length // RADIX
@@ -101,11 +104,17 @@
     def on_tm(device):
         return {"tm": device}
 
+    def wide(s):
+        return {"pairs": (me + s) % blocks, "tm": (mine + CORES * (s // blocks)) % tm}
+
     barrier = pltpu.get_barrier_semaphore()
     for s in range(1, blocks):
         pl.semaphore_signal(barrier, inc=1, device_id=on_pairs((me + s) % blocks), device_id_type=MESH)
     for s in range(1, tm):
         pl.semaphore_signal(barrier, inc=1, device_id=on_tm((mine + s) % tm), device_id_type=MESH)
+    for s in range(blocks, blocks * chips):
+        if s % blocks:
+            pl.semaphore_signal(barrier, inc=1, device_id=wide(s), device_id_type=MESH)
     for i in range(1, 8):
         x_copy(i).start()
 
@@ -135,6 +144,15 @@
     def last_copy(c, s):
         to = on_tm((mine + s) % tm)
         return remote(pack_in.at[c, mine], pack_in.at[c, mine], last_s.at[c, s], last_r.at[c, s], to)
+
+    def wide_copy(s):
+        c, to = chunks - 1, (me + s) % blocks
+        return remote(pack_out.at[c, to], pack_in.at[c, mine, me], wide_s.at[s], wide_r.at[s], wide(s))
+
+    def core_copy(k):
+        core = mine % CORES
+        at = pack_in.at[chunks - 1, CORES * k + core]
+        return remote(at, at, core_s.at[k], core_r.at[k], on_tm(mine + 1 - 2 * core))
 
     def each(low, high, act):
         def body(s, c):
@@ -179,7 +197,7 @@
     lax.fori_loop(0, 8, fold, 0)
     water[...] = jnp.zeros_like(water)
 
-    pl.semaphore_wait(barrier, blocks + tm - 2)
+    pl.semaphore_wait(barrier, (blocks - 1) * chips + tm - 1)
     pairs_copy.wait()
     ends[...] = jnp.zeros_like(ends)
     ends[0:1, 0:64] = pairs[0:1, :].astype(F32)
@@ -306,15 +324,25 @@
             return c
 
         lax.fori_loop(0, blocks // 2, pack, 0)
-        each(1, blocks, lambda s: pack_copy(part, s).start())
+        if part == chunks - 1:
+            each(1, blocks * chips, lambda s: wide_copy(s).start())
+        else:
+            each(1, blocks, lambda s: pack_copy(part, s).start())
         pack_in[part, mine, me] = pack_out[part, me]
 
     def share_chunk(part):
-        each(1, blocks, lambda s: pack_copy(part, s).wait())
-        each(1, tm, lambda s: last_copy(part, s).start())
+        if part == chunks - 1:
+            each(1, blocks * chips, lambda s: wide_copy(s).wait())
+            each(0, chips, lambda k: core_copy(k).start())
+        else:
+            each(1, blocks, lambda s: pack_copy(part, s).wait())
+            each(1, tm, lambda s: last_copy(part, s).start())
 
     def lag_chunk(part):
-        each(1, tm, lambda s: last_copy(part, s).wait())
+        if part == chunks - 1:
+            each(0, chips, lambda k: core_copy(k).wait())
+        else:
+            each(1, tm, lambda s: last_copy(part, s).wait())
         count = tm * blocks * half
         at = slice(part * count, (part + 1) * count)
         stacked = pack_in[part].reshape(count, 128).astype(F32)
@@ -397,6 +425,8 @@
             dma((chunks, tm)), dma((chunks, tm)),
             dma((chunks, blocks)), dma((chunks, blocks)),
             dma((chunks, tm)), dma((chunks, tm)),
+            dma((blocks * tm // CORES,)), dma((blocks * tm // CORES,)),
+            dma((tm // CORES,)), dma((tm // CORES,)),
         ],
         compiler_params=pltpu.CompilerParams(
             collective_id=0, has_side_effects=True, vmem_limit_bytes=56 * 1024 * 1024

time: 45.2 us -> 45.7 us (1.011)
  Pallas kernels: 43.5 us -> 44 us
    pallas_call x1, Pallas kernels: 43.5 us -> 44 us  [on_device(): pl.pallas_call(functools.partial(kernel, blocks, tm), out_shape=jax.Shape...]
where the time goes in v5:
time: 45.7 us; the launch traced here: 45.6 us
  Pallas kernels  44 us (96%)
  other arithmetic  1.57 us (3%)
    pallas_call x1, Pallas kernels, on_device(): pl.pallas_call(functools.partial(kernel, blocks, tm), out_shape=jax.Shape...  44 us
    mul x1, other arithmetic, on_device(): return result.T * scale  1.57 us

profile of v5, /device:TPU:0, one launch (start us, length us, event | category | flops | bytes accessed | tf_op | source)
XLA Modules:
  0.0 45.6 jit_solution(15674697336951962055)
XLA Ops:
  0.0 44.0 %shard_map.73 = f32[64,512]{1,0:T(8,128)} custom-call(f32[128,6144]{1,0:T(8,128)} %bitcast.5, f32[8,768]{1,0:T(8,128)} %constant.10.clone.hann_hbm, s32[1,512]{1,0:T(1,128)} %bitcast.6, s32[2,64]{1,0:T(2,128)} %bitcast.7, bf16[8,384,768]{2,1,0:T(8,128)(2,1)} %constant.11.clone.tab_hbm, bf16[3,512,1024]{2,1,0:T(8,128)(2,1)} %constant.12.clone.lag_hbm, ...), custom_call_target="tpu_custom_call" | custom-call | tf_op jit(solution)/shard_map/pallas_call | solution.py:393
  44.0 1.6 %multiply_bitcast_fusion = f32[512,64]{0,1:T(8,128)} fusion(f32[64,512]{1,0:T(8,128)} %shard_map.73), kind=kLoop, calls=%fused_computation | loop fusion | flops 32768 | bytes 262144 | tf_op jit(solution)/shard_map/mul | solution.py:438

commit v6 on v4

--- a/solution.py
+++ b/solution.py
@@ -67,6 +67,10 @@
     part_s, part_r, pack_s, pack_r, last_s, last_r,
 ):
     me, mine = lax.axis_index("pairs"), lax.axis_index("tm")
+    def wrapped(base, size):
+        return [jnp.where(base + s >= size, base + s - size, base + s) for s in range(size)]
+
+    block_at, tm_at = wrapped(me, blocks), wrapped(mine, tm)
     bins_each, chunks, bins, half = split(blocks, tm)
     chunk = bins_each // chunks
     group = blocks // RADIX
@@ -93,7 +97,7 @@
         return 1 + (i + blocks // 2 - 1) % (blocks - 1)
 
     def table_copy(s):
-        return pltpu.make_async_copy(tab_hbm.at[(me + s) % blocks], tab.at[s], tab_sem.at[s])
+        return pltpu.make_async_copy(tab_hbm.at[block_at[s]], tab.at[s], tab_sem.at[s])
 
     def on_pairs(device):
         return {"pairs": device}
@@ -103,11 +107,14 @@
 
     barrier = pltpu.get_barrier_semaphore()
     for s in range(1, blocks):
-        pl.semaphore_signal(barrier, inc=1, device_id=on_pairs((me + s) % blocks), device_id_type=MESH)
+        pl.semaphore_signal(barrier, inc=1, device_id=on_pairs(block_at[s]), device_id_type=MESH)
     for s in range(1, tm):
-        pl.semaphore_signal(barrier, inc=1, device_id=on_tm((mine + s) % tm), device_id_type=MESH)
+        pl.semaphore_signal(barrier, inc=1, device_id=on_tm(tm_at[s]), device_id_type=MESH)
     for i in range(1, 8):
         x_copy(i).start()
+    for i in range(blocks - 1):
+        table_copy(step_of(i)).start()
+    table_copy(0).start()
 
     def remote(src, dst, send, recv, device):
         return pltpu.make_async_remote_copy(
@@ -115,32 +122,30 @@
         )
 
     def ends_copy(s):
-        return remote(ends, ends_in.at[me], ends_s.at[s], ends_r.at[s], on_pairs((me + s) % blocks))
+        return remote(ends, ends_in.at[me], ends_s.at[s], ends_r.at[s], on_pairs(block_at[s]))
 
     def spec_copy(c, s):
-        to = on_pairs((me + s) % blocks)
+        to = on_pairs(block_at[s])
         return remote(spec_out.at[c, s], spec_in.at[c, me], spec_s.at[c, s], spec_r.at[c, s], to)
 
     def water_copy(s):
-        return remote(water, water_in.at[me], water_s.at[s], water_r.at[s], on_pairs((me + s) % blocks))
+        return remote(water, water_in.at[me], water_s.at[s], water_r.at[s], on_pairs(block_at[s]))
 
     def part_copy(c, s):
-        to = (mine + s) % tm
+        to = tm_at[s]
         return remote(part_out.at[c, to], part_in.at[c, mine], part_s.at[c, s], part_r.at[c, s], on_tm(to))
 
     def pack_copy(c, s):
-        to = (me + s) % blocks
+        to = block_at[s]
         return remote(pack_out.at[c, to], pack_in.at[c, mine, me], pack_s.at[c, s], pack_r.at[c, s], on_pairs(to))
 
     def last_copy(c, s):
-        to = on_tm((mine + s) % tm)
+        to = on_tm(tm_at[s])
         return remote(pack_in.at[c, mine], pack_in.at[c, mine], last_s.at[c, s], last_r.at[c, s], to)
 
     def each(low, high, act):
-        def body(s, c):
+        for s in range(low, high):
             act(s)
-            return c
-        lax.fori_loop(low, high, body, 0)
 
     hann_copy.wait()
     root = math.sqrt(0.5)
@@ -149,9 +154,6 @@
         low = pl.ds(pl.multiple_of(i * 16, 16), 16)
         high = pl.ds(pl.multiple_of(128 + i * 16, 16), 16)
         x_copy(i).wait()
-        for k in range(group):
-            at = i * group + k
-            table_copy(jnp.where(at < blocks - 1, step_of(at), 0)).start()
         mean = jnp.sum(x[low, :], axis=1, keepdims=True) * (1.0 / length)
         for k in range(short // 128):
             v = []
@@ -189,7 +191,7 @@
 
     def spectrum(s):
         table_copy(s).wait()
-        to = (me + s) % blocks
+        to = block_at[s]
         product = lax.dot_general(
             tab[s], folded[to // group], (((1,), (1,)), ((), ())), preferred_element_type=F32
         )
@@ -198,16 +200,15 @@
         water[...] += jnp.broadcast_to(jnp.sum(re * re + im * im, axis=0, keepdims=True), water.shape)
         return re.astype(BF16), im.astype(BF16)
 
-    def send_block(i, c):
-        s = step_of(i)
+    def send_block(s):
         re, im = spectrum(s)
         for part in range(chunks):
             spec_out[part, s, :chunk] = re[part * chunk:(part + 1) * chunk]
             spec_out[part, s, chunk:] = im[part * chunk:(part + 1) * chunk]
         spec_copy(0, s).start()
-        return c
-
-    lax.fori_loop(0, blocks - 1, send_block, 0)
+
+    for i in range(blocks - 1):
+        send_block(step_of(i))
     re, im = spectrum(0)
     for part in range(chunks):
         spec_in[part, me, :chunk] = re[part * chunk:(part + 1) * chunk]
@@ -215,14 +216,14 @@
     water_in[me] = water[...]
     each(1, blocks, lambda s: water_copy(s).start())
 
-    def send_next(part):
-        def body(i, c):
+    def send_next(part, low=0, high=blocks - 1):
+        for i in range(low, high):
             s = step_of(i)
             spec_copy(part, s).wait_send()
             if part + 1 < chunks:
                 spec_copy(part + 1, s).start()
-            return c
-        lax.fori_loop(0, blocks - 1, body, 0)
+
+    send_next(0, 0, blocks // 2)
 
     slot_copy.wait()
     for k in range(stations // 128):
@@ -245,7 +246,7 @@
         onehot[g] = jnp.where(row_ids == slots, 1.0, 0.0).astype(BF16)
         return c
 
-    lax.fori_loop(0, blocks // 2, pick, 0)
+    lax.fori_loop(0, blocks // 2, pick, 0, unroll=2)
 
     if half > bins:
         part_out[...] = jnp.zeros_like(part_out)
@@ -270,7 +271,7 @@
                 white[at:at + chunk, cols] = second.astype(BF16)
             return c
 
-        lax.fori_loop(0, blocks // 2, whiten_two, 0)
+        lax.fori_loop(0, blocks // 2, whiten_two, 0, unroll=2)
 
         def cross(g, c):
             got = jnp.dot(white[...], onehot[g], preferred_element_type=F32)
@@ -289,7 +290,7 @@
                 part_out[part, t, g, half:half + bins] = imag[rows].astype(BF16)
             return c
 
-        lax.fori_loop(0, blocks // 2, cross, 0)
+        lax.fori_loop(0, blocks // 2, cross, 0, unroll=4)
         each(1, tm, lambda s: part_copy(part, s).start())
         part_in[part, mine] = part_out[part, mine]
 
@@ -305,7 +306,7 @@
             pack_out[part, 2 * g + 1] = jnp.where(lane < 64, swap(top), bottom).astype(BF16)
             return c
 
-        lax.fori_loop(0, blocks // 2, pack, 0)
+        lax.fori_loop(0, blocks // 2, pack, 0, unroll=4)
         each(1, blocks, lambda s: pack_copy(part, s).start())
         pack_in[part, mine, me] = pack_out[part, me]
 
@@ -325,7 +326,7 @@
 
     lag_copy.start()
     turn_copy.start()
-    send_next(0)
+    send_next(0, blocks // 2)
     each(1, blocks, lambda s: water_copy(s).wait())
     for part in range(chunks):
         each(1, blocks, lambda s: spec_copy(part, s).wait_recv())

time: 45.2 us -> 44.9 us (level)
  no operation moved by 1% of the time
where the time goes in v6:
time: 44.9 us; the launch traced here: 44.8 us
  Pallas kernels  43.2 us (96%)
  other arithmetic  1.57 us (3%)
    pallas_call x1, Pallas kernels, on_device(): pl.pallas_call(functools.partial(kernel, blocks, tm), out_shape=jax.Shape...  43.2 us
    mul x1, other arithmetic, on_device(): return result.T * scale  1.57 us

profile of v6, /device:TPU:0, one launch (start us, length us, event | category | flops | bytes accessed | tf_op | source)
XLA Modules:
  0.0 44.8 jit_solution(7253408789758132326)
XLA Ops:
  0.0 43.2 %shard_map.73 = f32[64,512]{1,0:T(8,128)} custom-call(f32[128,6144]{1,0:T(8,128)} %bitcast.5, f32[8,768]{1,0:T(8,128)} %constant.10.clone.hann_hbm, s32[1,512]{1,0:T(1,128)} %bitcast.6, s32[2,64]{1,0:T(2,128)} %bitcast.7, bf16[8,384,768]{2,1,0:T(8,128)(2,1)} %constant.11.clone.tab_hbm, bf16[3,512,1024]{2,1,0:T(8,128)(2,1)} %constant.12.clone.lag_hbm, ...), custom_call_target="tpu_custom_call" | custom-call | tf_op jit(solution)/shard_map/pallas_call | solution.py:366
  43.2 1.6 %multiply_bitcast_fusion = f32[512,64]{0,1:T(8,128)} fusion(f32[64,512]{1,0:T(8,128)} %shard_map.73), kind=kLoop, calls=%fused_computation | loop fusion | flops 32768 | bytes 262144 | tf_op jit(solution)/shard_map/mul | solution.py:409

commit v7 on v6

--- a/solution.py
+++ b/solution.py
@@ -216,14 +216,10 @@
     water_in[me] = water[...]
     each(1, blocks, lambda s: water_copy(s).start())
 
-    def send_next(part, low=0, high=blocks - 1):
-        for i in range(low, high):
-            s = step_of(i)
-            spec_copy(part, s).wait_send()
-            if part + 1 < chunks:
-                spec_copy(part + 1, s).start()
-
-    send_next(0, 0, blocks // 2)
+    order = [step_of(i) for i in range(blocks - 1)]
+    for part in range(1, min(chunks, 2)):
+        for s in order:
+            spec_copy(part, s).start()
 
     slot_copy.wait()
     for k in range(stations // 128):
@@ -326,23 +322,30 @@
 
     lag_copy.start()
     turn_copy.start()
-    send_next(0, blocks // 2)
-    each(1, blocks, lambda s: water_copy(s).wait())
+    for part in range(2, chunks):
+        for s in order:
+            spec_copy(part - 2, s).wait_send()
+            spec_copy(part, s).start()
+    each(1, blocks, lambda s: water_copy(s).wait_recv())
     for part in range(chunks):
         each(1, blocks, lambda s: spec_copy(part, s).wait_recv())
         cross_chunk(part)
-        if part + 1 < chunks:
-            send_next(part + 1)
-        if part == 0:
-            lag_copy.wait()
-            turn_copy.wait()
-        else:
+        if 0 < part < chunks - 1:
             share_chunk(part - 1)
         pack_chunk(part)
-    for part in range(chunks - 1):
+    lag_copy.wait()
+    turn_copy.wait()
+    if chunks > 1:
+        share_chunk(chunks - 2)
+    for part in range(chunks - 2):
         lag_chunk(part)
     share_chunk(chunks - 1)
-    lag_chunk(chunks - 1)
+    for part in range(max(0, chunks - 2), chunks):
+        lag_chunk(part)
+    for part in range(max(0, chunks - 2), chunks):
+        for s in order:
+            spec_copy(part, s).wait_send()
+    each(1, blocks, lambda s: water_copy(s).wait_send())
     out[...] = total_out[...].T[:64]
 
 

time: 44.9 us -> 44.7 us (level)
  no operation moved by 1% of the time
where the time goes in v7:
time: 44.7 us; the launch traced here: 44.6 us
  Pallas kernels  43 us (96%)
  other arithmetic  1.57 us (4%)
    pallas_call x1, Pallas kernels, on_device(): pl.pallas_call(functools.partial(kernel, blocks, tm), out_shape=jax.Shape...  43 us
    mul x1, other arithmetic, on_device(): return result.T * scale  1.57 us

profile of v7, /device:TPU:0, one launch (start us, length us, event | category | flops | bytes accessed | tf_op | source)
XLA Modules:
  0.0 44.6 jit_solution(8492388454461706916)
XLA Ops:
  0.0 43.0 %shard_map.73 = f32[64,512]{1,0:T(8,128)} custom-call(f32[128,6144]{1,0:T(8,128)} %bitcast.5, f32[8,768]{1,0:T(8,128)} %constant.10.clone.hann_hbm, s32[1,512]{1,0:T(1,128)} %bitcast.6, s32[2,64]{1,0:T(2,128)} %bitcast.7, bf16[8,384,768]{2,1,0:T(8,128)(2,1)} %constant.11.clone.tab_hbm, bf16[3,512,1024]{2,1,0:T(8,128)(2,1)} %constant.12.clone.lag_hbm, ...), custom_call_target="tpu_custom_call" | custom-call | tf_op jit(solution)/shard_map/pallas_call | solution.py:369
  43.0 1.6 %multiply_bitcast_fusion = f32[512,64]{0,1:T(8,128)} fusion(f32[64,512]{1,0:T(8,128)} %shard_map.73), kind=kLoop, calls=%fused_computation | loop fusion | flops 32768 | bytes 262144 | tf_op jit(solution)/shard_map/mul | solution.py:412

commit v8 on v7

--- a/solution.py
+++ b/solution.py
@@ -21,9 +21,7 @@
 
 def split(blocks, tm):
     bins_each = F // blocks
-    chunks = max(1, bins_each // (16 * tm))
-    while bins_each % (chunks * tm):
-        chunks -= 1
+    chunks = 1
     bins = bins_each // (chunks * tm)
     return bins_each, chunks, bins, -(-bins // 16) * 16
 
@@ -147,6 +145,8 @@
         for s in range(low, high):
             act(s)
 
+    for r in (0, RADIX // 2):
+        folded[r, 128:, :] = jnp.zeros((128, short), BF16)
     hann_copy.wait()
     root = math.sqrt(0.5)
 
@@ -167,15 +167,15 @@
             a2, b2 = u[0] - u[2], u[3] - u[1]
             a1, b1 = d[0] + dm, -d[2] - dp
             a3, b3 = d[0] - dm, d[2] - dp
-            zero = jnp.zeros_like(even)
             classes = [
-                (even + odd, zero), (a1, b1), (a2, b2), (a3, b3),
-                (even - odd, zero), (a3, -b3), (a2, -b2), (a1, -b1),
+                (even + odd, None), (a1, b1), (a2, b2), (a3, b3),
+                (even - odd, None), (a3, -b3), (a2, -b2), (a1, -b1),
             ]
             cols = slice(k * 128, (k + 1) * 128)
             for r, (a, b) in enumerate(classes):
                 folded[r, low, cols] = a.astype(BF16)
-                folded[r, high, cols] = b.astype(BF16)
+                if b is not None:
+                    folded[r, high, cols] = b.astype(BF16)
         return c
 
     lax.fori_loop(0, 8, fold, 0)

time: 44.7 us -> 48.7 us (1.089)
  Pallas kernels: 43 us -> 46.6 us
    pallas_call x1, Pallas kernels: 43 us -> 46.6 us  [on_device(): pl.pallas_call(functools.partial(kernel, blocks, tm), out_shape=jax.Shape...]
where the time goes in v8:
time: 48.7 us; the launch traced here: 48.2 us
  Pallas kernels  46.6 us (96%)
  other arithmetic  1.57 us (3%)
    pallas_call x1, Pallas kernels, on_device(): pl.pallas_call(functools.partial(kernel, blocks, tm), out_shape=jax.Shape...  46.6 us
    mul x1, other arithmetic, on_device(): return result.T * scale  1.57 us

profile of v8, /device:TPU:0, one launch (start us, length us, event | category | flops | bytes accessed | tf_op | source)
XLA Modules:
  0.0 48.2 jit_solution(9176735237009798212)
XLA Ops:
  0.0 46.6 %shard_map.73 = f32[64,512]{1,0:T(8,128)} custom-call(f32[128,6144]{1,0:T(8,128)} %bitcast.5, f32[8,768]{1,0:T(8,128)} %constant.10.clone.hann_hbm, s32[1,512]{1,0:T(1,128)} %bitcast.6, s32[2,64]{1,0:T(2,128)} %bitcast.7, bf16[8,384,768]{2,1,0:T(8,128)(2,1)} %constant.11.clone.tab_hbm, bf16[1,512,3072]{2,1,0:T(8,128)(2,1)} %constant.12.clone.lag_hbm, ...), custom_call_target="tpu_custom_call" | custom-call | tf_op jit(solution)/shard_map/pallas_call | solution.py:369
  46.6 1.6 %multiply_bitcast_fusion = f32[512,64]{0,1:T(8,128)} fusion(f32[64,512]{1,0:T(8,128)} %shard_map.73), kind=kLoop, calls=%fused_computation | loop fusion | flops 32768 | bytes 262144 | tf_op jit(solution)/shard_map/mul | solution.py:412

commit v9 on v8

--- a/solution.py
+++ b/solution.py
@@ -21,7 +21,9 @@
 
 def split(blocks, tm):
     bins_each = F // blocks
-    chunks = 1
+    chunks = max(1, bins_each // (16 * tm))
+    while bins_each % (chunks * tm):
+        chunks -= 1
     bins = bins_each // (chunks * tm)
     return bins_each, chunks, bins, -(-bins // 16) * 16
 
@@ -59,7 +61,7 @@
 def kernel(
     blocks, tm,
     x_hbm, hann_hbm, slot_hbm, pairs_hbm, tab_hbm, lag_hbm, turn_hbm, out,
-    x, hann, slot_row, pairs, tab, lag, slot_col, ends, folded, water, spec_out, spec_in, water_in, ends_in, onehot, white,
+    x, means, hann, slot_row, pairs, tab, lag, slot_col, ends, folded, water, spec_out, spec_in, water_in, ends_in, onehot, white,
     part_out, part_in, pack_out, pack_in, turn, total_out,
     local_sem, x_sem, tab_sem, ends_s, ends_r, spec_s, spec_r, water_s, water_r,
     part_s, part_r, pack_s, pack_r, last_s, last_r,
@@ -148,13 +150,17 @@
     for r in (0, RADIX // 2):
         folded[r, 128:, :] = jnp.zeros((128, short), BF16)
     hann_copy.wait()
+    for i in range(8):
+        x_copy(i).wait()
+        at = slice(i * 16, (i + 1) * 16)
+        mean = jnp.sum(x[at, :], axis=1, keepdims=True) * (1.0 / length)
+        means[at, :] = jnp.broadcast_to(mean, (16, 128))
     root = math.sqrt(0.5)
 
     def fold(i, c):
         low = pl.ds(pl.multiple_of(i * 16, 16), 16)
         high = pl.ds(pl.multiple_of(128 + i * 16, 16), 16)
-        x_copy(i).wait()
-        mean = jnp.sum(x[low, :], axis=1, keepdims=True) * (1.0 / length)
+        mean = means[low, :]
         for k in range(short // 128):
             v = []
             for q in range(RADIX):
@@ -178,7 +184,7 @@
                     folded[r, high, cols] = b.astype(BF16)
         return c
 
-    lax.fori_loop(0, 8, fold, 0)
+    lax.fori_loop(0, 8, fold, 0, unroll=2)
     water[...] = jnp.zeros_like(water)
 
     pl.semaphore_wait(barrier, blocks + tm - 2)
@@ -373,6 +379,7 @@
         out_specs=vmem,
         scratch_shapes=[
             pltpu.VMEM((128, length), F32),
+            pltpu.VMEM((128, 128), F32),
             pltpu.VMEM((RADIX, short), F32),
             pltpu.VMEM((1, stations), jnp.int32),
             pltpu.VMEM((2, pairs_each), jnp.int32),

time: 48.7 us -> 45.3 us (0.930)
  Pallas kernels: 46.6 us -> 43.6 us
    pallas_call x1, Pallas kernels: 46.6 us -> 43.6 us  [on_device(): pl.pallas_call(functools.partial(kernel, blocks, tm), out_shape=jax.Shape...]
where the time goes in v9:
time: 45.3 us; the launch traced here: 45.2 us
  Pallas kernels  43.6 us (96%)
  other arithmetic  1.57 us (3%)
    pallas_call x1, Pallas kernels, on_device(): pl.pallas_call(functools.partial(kernel, blocks, tm), out_shape=jax.Shape...  43.6 us
    mul x1, other arithmetic, on_device(): return result.T * scale  1.57 us

profile of v9, /device:TPU:0, one launch (start us, length us, event | category | flops | bytes accessed | tf_op | source)
XLA Modules:
  0.0 45.2 jit_solution(9132937266290309138)
XLA Ops:
  0.0 43.6 %shard_map.73 = f32[64,512]{1,0:T(8,128)} custom-call(f32[128,6144]{1,0:T(8,128)} %bitcast.5, f32[8,768]{1,0:T(8,128)} %constant.10.clone.hann_hbm, s32[1,512]{1,0:T(1,128)} %bitcast.6, s32[2,64]{1,0:T(2,128)} %bitcast.7, bf16[8,384,768]{2,1,0:T(8,128)(2,1)} %constant.11.clone.tab_hbm, bf16[3,512,1024]{2,1,0:T(8,128)(2,1)} %constant.12.clone.lag_hbm, ...), custom_call_target="tpu_custom_call" | custom-call | tf_op jit(solution)/shard_map/pallas_call | solution.py:375
  43.6 1.6 %multiply_bitcast_fusion = f32[512,64]{0,1:T(8,128)} fusion(f32[64,512]{1,0:T(8,128)} %shard_map.73), kind=kLoop, calls=%fused_computation | loop fusion | flops 32768 | bytes 262144 | tf_op jit(solution)/shard_map/mul | solution.py:419
